TPU v7x, 256 devices: a whole 4x4x8 slice. The times are simulated.
256 devices in a mesh: section: 2 (over y_lo), head: 8 (over x, core), row: 16 (over z, y_hi).
Axes of the slice: x: 4, y: 4 (y_hi: 2, y_lo: 2; y = y_hi * 2 + y_lo), z: 8, core: 2. Of those that a mesh axis runs over, the one named last changes fastest.
Arguments:
- hidden: bfloat16 [2, 512, 8192], P('section', 'row'), may hold values from -6 to 6
- attn_gain: float32 [8192], replicated, may hold values from 0.1 to 1.9
- kv_weight: bfloat16 [8192, 2048], P(None, 'head'), may hold values from -0.0625 to 0.0625
- queries: bfloat16 [2, 512, 8192], P('section', 'row', 'head'), may hold values from -6 to 6
- cache_kv: bfloat16 [512, 768, 2048], P('row', None, 'head'), may hold values from -6 to 6
- lengths: int32 [512], P('row'), may hold values from 1 to 768, 196608 in all
- block_owner: int32 [128], replicated, may hold values from 0 to 511
- out_weight: bfloat16 [8192, 8192], P('head', 'row'), may hold values from -0.16572815 to 0.16572815
- final_gain: float32 [8192], replicated, may hold values from 0.1 to 1.9
- vocab_weight: bfloat16 [8192, 65536], P(None, ('section', 'head', 'row')), may hold values from -0.24 to 0.24
Outputs:
- layer_out: bfloat16 [2, 512, 8192], P('section', 'row')
- entropy: float32 [512], replicated
Inputs may be any that keep to these rules, and one draw needn't show every extreme that they name: `lengths`: every draw has a row whose cache holds exactly 768 live positions.
All inputs are finite; a program needn't handle non-finite values. No bound on the sum of `lengths` on one device may be relied on, other than what follows from the above.
Results may differ from a plain program's by a relative error of at most 0.0055.
Values may be sent and summed in bfloat16 or wider, within the bound.
A program may use at most 128 MiB of HBM per device.

v0:
```python
import math

import jax
import jax.numpy as jnp
from jax import lax
from jax.sharding import PartitionSpec as P

BLK = 4


NORM_EPSILON = 1e-05


def from_behind(value, axis, steps):
    count = lax.axis_size(axis)
    first, last = (max(0, -steps), min(count, count - steps))
    return lax.ppermute(value, axis, [(source, source + steps) for source in range(first, last)])


def from_root(array, axis, root):
    mine = lax.axis_index(axis) == root
    return lax.psum(jnp.where(mine, array, jnp.zeros_like(array)), axis)


def rms_scale(values, gain):
    wide = values.astype(jnp.float32)
    spread = jnp.mean(wide * wide, axis=-1, keepdims=True)
    return wide * lax.rsqrt(spread + NORM_EPSILON) * gain


def body(
    hidden,
    attn_gain,
    kv_weight,
    queries,
    cache_kv,
    lengths,
    block_owner,
    out_weight,
    final_gain,
    vocab_weight,
):
    tokens = hidden.shape[1]
    head_dim = kv_weight.shape[1] // 2
    group_size = queries.shape[2] // head_dim
    cache_len = cache_kv.shape[1]
    score_scale = 1.0 / math.sqrt(head_dim)
    is_decode = lax.axis_index("section") == 1
    first_row = lax.axis_index("row") * tokens
    rows_here = first_row + jnp.arange(tokens, dtype=jnp.int32)
    normed = rms_scale(hidden[0], attn_gain).astype(jnp.bfloat16)
    fresh_kv = jnp.dot(normed, kv_weight, preferred_element_type=jnp.float32).astype(jnp.bfloat16)
    arrived = from_behind(fresh_kv, "section", 1)
    prompt_here = jnp.where(is_decode, arrived, fresh_kv)
    prompt_all = lax.all_gather(prompt_here, "row", axis=0, tiled=True)
    prompt_keys = prompt_all[:, :head_dim]
    prompt_vals = prompt_all[:, head_dim:]
    total_prompt = prompt_all.shape[0]
    asked_rows = queries[0].reshape(tokens, group_size, head_dim)
    token_index = jnp.arange(total_prompt, dtype=jnp.int32)
    owners = jnp.repeat(block_owner, BLK)
    prompt_mask = jnp.where(
        is_decode, owners[None, :] == rows_here[:, None], token_index[None, :] <= rows_here[:, None]
    )
    block_scores = (
        jnp.einsum("igd,td->igt", asked_rows, prompt_keys, preferred_element_type=jnp.float32)
        * score_scale
    )
    block_scores = jnp.where(prompt_mask[:, None, :], block_scores, -jnp.inf)
    own_scores = (
        jnp.einsum(
            "igd,id->ig", asked_rows, fresh_kv[:, :head_dim], preferred_element_type=jnp.float32
        )
        * score_scale
    )
    own_scores = jnp.where(is_decode, own_scores, -jnp.inf)
    cache_keys = cache_kv[:, :, :head_dim]
    cache_vals = cache_kv[:, :, head_dim:]

    def cache_scores_live():
        scores = (
            jnp.einsum("igd,icd->igc", asked_rows, cache_keys, preferred_element_type=jnp.float32)
            * score_scale
        )
        live = jnp.arange(cache_len, dtype=jnp.int32)[None, :] < lengths[:, None]
        return jnp.where(live[:, None, :], scores, -jnp.inf)

    def cache_scores_none():
        return jnp.full((tokens, group_size, cache_len), -jnp.inf, jnp.float32)

    cache_scores = lax.cond(is_decode, cache_scores_live, cache_scores_none)
    top_score = jnp.maximum(
        jnp.maximum(jnp.max(cache_scores, axis=-1), jnp.max(block_scores, axis=-1)), own_scores
    )
    cache_weights = jnp.exp(cache_scores - top_score[..., None])
    block_weights = jnp.exp(block_scores - top_score[..., None])
    own_weights = jnp.exp(own_scores - top_score)
    weight_sum = jnp.sum(cache_weights, axis=-1) + jnp.sum(block_weights, axis=-1) + own_weights
    cache_rounded = cache_weights.astype(jnp.bfloat16)

    def cache_values_live():
        return jnp.einsum(
            "igc,icd->igd", cache_rounded, cache_vals, preferred_element_type=jnp.float32
        )

    def cache_values_none():
        return jnp.zeros((tokens, group_size, head_dim), jnp.float32)

    gathered = lax.cond(is_decode, cache_values_live, cache_values_none)
    gathered = gathered + jnp.einsum(
        "igt,td->igd",
        block_weights.astype(jnp.bfloat16),
        prompt_vals,
        preferred_element_type=jnp.float32,
    )
    own_rounded = own_weights.astype(jnp.bfloat16).astype(jnp.float32)
    gathered = gathered + own_rounded[..., None] * fresh_kv[:, None, head_dim:].astype(jnp.float32)
    attention = (
        (gathered / weight_sum[..., None])
        .astype(jnp.bfloat16)
        .reshape(tokens, group_size * head_dim)
    )
    partial_out = jnp.dot(
        lax.all_gather(attention, "row", axis=0, tiled=True),
        out_weight,
        preferred_element_type=jnp.float32,
    )
    summed = lax.psum(partial_out, "head")
    columns = lax.all_to_all(summed, "row", split_axis=0, concat_axis=1, tiled=True)
    layer_out = (hidden[0].astype(jnp.float32) + columns).astype(jnp.bfloat16)
    final_rows = rms_scale(layer_out, final_gain).astype(jnp.bfloat16)
    every_row = lax.all_gather(final_rows, "row", axis=0, tiled=True)
    every_row = from_root(every_row, "section", 1)
    logits = jnp.dot(every_row, vocab_weight, preferred_element_type=jnp.float32)
    local_top = jnp.max(logits, axis=1)
    top_logit = lax.pmax(local_top, ("section", "head", "row"))
    shifted = logits - top_logit[:, None]
    exponent_terms = jnp.exp(shifted)
    total_mass, moment = lax.psum(
        (jnp.sum(exponent_terms, axis=1), jnp.sum(exponent_terms * shifted, axis=1)),
        ("section", "head", "row"),
    )
    entropy = jnp.log(total_mass) - moment / total_mass
    return (layer_out[None], entropy)


def solution(mesh):
    return jax.shard_map(
        body,
        mesh=mesh,
        in_specs=(
            P("section", "row", None),
            P(),
            P(None, "head"),
            P("section", "row", "head"),
            P("row", None, "head"),
            P("row"),
            P(),
            P("head", "row"),
            P(),
            P(None, ("section", "head", "row")),
        ),
        out_specs=(P("section", "row", None), P()),
        check_vma=False,
    )
```

profile of v0, /device:TPU:1, one launch (start us, length us, event | category | flops | bytes accessed | tf_op | source)
XLA Modules:
  0.0 765.1 jit_solution(12306446683461868149)
XLA Ops:
  7.2 0.0 copy-start
  7.2 0.0 all-gather.3.cloned.1.call-start
  7.2 1.3 fusion.15
  8.6 3.2 convolution_convert_fusion
  11.8 4.0 collective-permute-start
  15.9 0.9 copy.49
  16.7 0.7 broadcast_in_dim.35
  17.5 0.1 eq.24
  17.6 0.2 fusion.31
  17.7 0.1 fusion.30
  17.8 0.1 copy.45
  17.9 0.1 conditional.2
  17.9 0.1 broadcast.83
  18.0 0.0 collective-permute-done
  18.0 38.1 %all_gather.9 = bf16[512,256]{1,0:T(8,128)(2,1)S(1)} all-gather(bf16[32,256]{1,0:T(8,128)(2,1)S(1)} %broadcast_select_fusion.1), channel_id=1, replica_groups=mesh['section'=2,'head'=8,'row'=16] {'row'}, dimensions={0}, use_global_device_ids=true | all-gather | bytes 278528 | tf_op jit(solution)/shard_map/all_gather | solution.py:55
  56.1 0.3 fusion.35
  56.5 0.1 copy.36
  56.5 0.0 copy-start.1
  56.5 0.2 fusion.26
  56.8 0.1 copy.38
  56.8 0.3 fusion.20
  57.1 0.1 copy.39
  57.2 0.1 copy.40
  57.3 0.0 copy-start.2
  57.3 0.3 fusion.14
  57.6 0.6 copy.66
  58.3 0.0 all-gather.3.cloned.1.call-update
  58.3 0.0 all-reduce.4.cloned.1.call-start
  58.3 85.1 %all-gather.3.cloned.1.call-done = bf16[512,1024]{1,0:T(8,128)(2,1)} async-done(((bf16[32,1024]{1,0:T(8,128)(2,1)}), bf16[512,1024]{1,0:T(8,128)(2,1)}) %all-gather.3.cloned.1.call-update) | async-done | bytes 1048592 | tf_op jit(solution)/shard_map/all_gather | solution.py:124
  143.5 0.0 copy-done
  143.5 3.0 fusion.37
  146.4 0.0 all-reduce.4.cloned.1.call-update
  146.5 65.9 %all-reduce.4.cloned.1.call-done = f32[16,32,512]{2,1,0:T(8,128)} async-done(((f32[16,32,512]{2,1,0:T(8,128)}), f32[16,32,512]{2,1,0:T(8,128)}) %all-reduce.4.cloned.1.call-update) | async-done | bytes 1048592 | tf_op jit(solution)/shard_map/psum | solution.py:128
  212.4 9.3 %all-to-all-start = ((f32[16,32,512]{2,1,0:T(8,128)}), f32[16,32,512]{2,1,0:T(8,128)S(1)}, u32[]{:S(2)}, u32[]{:S(2)}) async-start(f32[16,32,512]{2,1,0:T(8,128)} %all-reduce.4.cloned.1.call-done), calls=%async_computation | async-start | bytes 2097152 | tf_op jit(solution)/shard_map/all_to_all | solution.py:129
  221.6 0.0 all-gather.5.cloned.1.call-start
  221.7 0.0 copy-done.1
  221.7 1.2 copy.51
  222.9 24.7 %all-to-all-done = f32[16,32,512]{2,1,0:T(8,128)S(1)} async-done(((f32[16,32,512]{2,1,0:T(8,128)}), f32[16,32,512]{2,1,0:T(8,128)S(1)}, u32[]{:S(2)}, u32[]{:S(2)}) %all-to-all-start) | async-done | bytes 1048608 | tf_op jit(solution)/shard_map/all_to_all | solution.py:129
  247.6 0.1 copy.48
  247.7 1.9 multiply_reduce_fusion
  249.7 0.0 copy-done.2
  249.7 1.0 multiply_convert_fusion
  250.7 0.0 all-gather.5.cloned.1.call-update
  250.7 0.0 all-reduce.6.cloned.1.call-start
  250.7 135.4 %all-gather.5.cloned.1.call-done = bf16[512,8192]{1,0:T(8,128)(2,1)} async-done(((bf16[32,8192]{1,0:T(8,128)(2,1)}), bf16[512,8192]{1,0:T(8,128)(2,1)}) %all-gather.5.cloned.1.call-update) | async-done | bytes 8388624 | tf_op jit(solution)/shard_map/all_gather | solution.py:132
  386.1 3.8 broadcast_select_fusion
  389.9 0.0 all-reduce.6.cloned.1.call-update
  389.9 1.6 copy.41
  391.5 1.4 all_to_all.19
  392.9 0.9 add_convert_fusion
  393.8 206.6 %all-reduce.6.cloned.1.call-done = bf16[512,8192]{1,0:T(8,128)(2,1)} async-done(((bf16[512,8192]{1,0:T(8,128)(2,1)}), bf16[512,8192]{1,0:T(8,128)(2,1)}) %all-reduce.6.cloned.1.call-update) | async-done | bytes 8388624 | tf_op jit(solution)/shard_map/psum | solution.py:22
  600.4 7.0 fusion.36
  607.3 77.4 %pmax.7 = f32[512]{0:T(512)S(1)} all-reduce(f32[512]{0:T(512)S(1)} %get-tuple-element.47), channel_id=1, replica_groups=mesh['section'=2,'head'=8,'row'=16] {'section','head','row'}, use_global_device_ids=true, to_apply=%region_13.14 | all-reduce | flops 512 | bytes 4096 | tf_op jit(solution)/shard_map/pmax | solution.py:136
  684.7 0.1 exponential_reduce_fusion
  684.8 73.2 %all-reduce = (f32[512]{0:T(512)S(1)}, f32[512]{0:T(512)S(1)}) all-reduce(f32[512]{0:T(512)S(1)} %get-tuple-element.32, f32[512]{0:T(512)S(1)} %get-tuple-element.31), channel_id=1, replica_groups=mesh['section'=2,'head'=8,'row'=16] {'section','head','row'}, use_global_device_ids=true, to_apply=%region_17.18 | all-reduce | flops 1024 | bytes 8192 | tf_op jit(solution)/shard_map/psum | solution.py:139
  758.0 0.6 divide_subtract_fusion
  (10 shorter events, 0.1 us)
Async XLA Ops:
  7.2 136.3 %copy-start = (bf16[1024,512]{1,0:T(8,128)(2,1)S(1)}, bf16[1024,512]{1,0:T(8,128)(2,1)}, u32[]{:S(2)}) copy-start(bf16[1024,512]{1,0:T(8,128)(2,1)} %param.21) | copy-start | bytes 3145732
  7.2 136.3 %all-gather.3.cloned.1.call-start = ((), (), s32[]{:S(2)}) async-start(), calls=%async_computation.1 | async-start | bytes 1114112 | tf_op jit(solution)/shard_map/all_gather | solution.py:124
  11.8 6.2 collective-permute-start
  56.5 165.2 %copy-start.1 = (bf16[1,32,8192]{2,1,0:T(8,128)(2,1)S(1)}, bf16[1,32,8192]{2,1,0:T(8,128)(2,1)}, u32[]{:S(2)}) copy-start(bf16[1,32,8192]{2,1,0:T(8,128)(2,1)} %param.14) | copy-start | bytes 1572868
  57.3 192.4 %copy-start.2 = (f32[8192]{0:T(1024)S(1)}, f32[8192]{0:T(1024)}, u32[]{:S(2)}) copy-start(f32[8192]{0:T(1024)} %param.22) | copy-start | bytes 98308
  58.3 154.1 %all-reduce.4.cloned.1.call-start = ((), (), s32[]{:S(2)}) async-start(), calls=%async_computation.2 | async-start | bytes 2097152 | tf_op jit(solution)/shard_map/psum | solution.py:128
  212.4 35.3 %all-to-all-start = ((f32[16,32,512]{2,1,0:T(8,128)}), f32[16,32,512]{2,1,0:T(8,128)S(1)}, u32[]{:S(2)}, u32[]{:S(2)}) async-start(f32[16,32,512]{2,1,0:T(8,128)} %all-reduce.4.cloned.1.call-done), calls=%async_computation | async-start | bytes 2097152 | tf_op jit(solution)/shard_map/all_to_all | solution.py:129
  221.6 164.5 %all-gather.5.cloned.1.call-start = ((), (), s32[]{:S(2)}) async-start(), calls=%async_computation.3 | async-start | bytes 8912896 | tf_op jit(solution)/shard_map/all_gather | solution.py:132
  250.7 349.7 %all-reduce.6.cloned.1.call-start = ((), (), s32[]{:S(2)}) async-start(), calls=%async_computation.4 | async-start | bytes 16777216 | tf_op jit(solution)/shard_map/psum | solution.py:22
Sparse Core Ops, SparseCore 0:
  58.4 85.0 all-gather.2
  146.6 65.7 all-reduce.3
  250.8 135.2 all-gather.4
  390.0 210.2 all-reduce.5
where the time goes:
time: 766 us; the launch traced here: 765 us
  waiting for transfers between devices  518 us (68%)
  blocking collectives  189 us (25%)
  matrix products  13.9 us (2%)
  between operations  13.9 us (2%)
  starting transfers between devices  13.5 us (2%)
  other arithmetic  10.2 us (1%)
    psum x1, waiting for transfers between devices, from_root(): return lax.psum(jnp.where(mine, array, jnp.zeros_like(array)), axis)  207 us
    all_gather x1, waiting for transfers between devices, body(): every_row = lax.all_gather(final_rows, 'row', axis=0, tiled=True)  135 us
    all_gather x1, waiting for transfers between devices, body(): lax.all_gather(attention, 'row', axis=0, tiled=True)  85.1 us
    pmax x1, blocking collectives, body(): top_logit = lax.pmax(local_top, ('section', 'head', 'row'))  77.4 us
    psum x1, blocking collectives, body(): lax.psum((jnp.sum(exponent_terms, axis=1), jnp.sum(exponent_terms * shift...  73.2 us
    psum x1, waiting for transfers between devices, body(): summed = lax.psum(partial_out, 'head')  65.9 us
    all_gather x1, blocking collectives, body(): prompt_all = lax.all_gather(prompt_here, 'row', axis=0, tiled=True)  38.1 us
    all_to_all x1, waiting for transfers between devices, body(): lax.all_to_all(summed, 'row', split_axis=0, concat_axis=1, tiled=True)  24.7 us
  transfers between devices with their start and end apart: 6, of which 5 were waited for; matrix products, arithmetic and copies ran while one was open for 1% of the time, Pallas kernels for 0%

commit v1 on v0

v1 whole, which is shorter than its diff:
```python
import functools
import math

import jax
import jax.numpy as jnp
from jax import lax
from jax.experimental import pallas as pl
from jax.experimental.pallas import tpu as pltpu
from jax.sharding import PartitionSpec as P

MESH = pl.DeviceIdType.MESH
BF = jnp.bfloat16
F32 = jnp.float32
EPS = 1e-05
NEG = -1e30
BLK = 4
NX, NY, NZ = 4, 4, 8
TOK = 32
COLS = 1024
CACHE_PARTS = 8
KV_PARTS = 4


def dot(a, b):
    return jnp.dot(a, b, preferred_element_type=F32)


def dot_t(a, b):
    return lax.dot_general(a, b, (((1,), (1,)), ((), ())), preferred_element_type=F32)


def wrap(value, n):
    return lax.rem(value + n, n)


class Place:
    def __init__(self):
        s, h, r = (lax.axis_index(a) for a in ("section", "head", "row"))
        self.s, self.h, self.r = s, h, r
        self.x, self.c = lax.div(h, 2), lax.rem(h, 2)
        self.z, self.yh = lax.div(r, 2), lax.rem(r, 2)
        self.y = self.yh * 2 + s
        self.decode = s == 1
        self.prefill = s == 0

    def at(self, x, y, z, c):
        return (lax.rem(y, 2), x * 2 + c, z * 2 + lax.div(y, 2))

    def off(self, dx=0, dy=0, dz=0, dc=0):
        x = wrap(self.x + dx, NX) if dx else self.x
        y = wrap(self.y + dy, NY) if dy else self.y
        z = wrap(self.z + dz, NZ) if dz else self.z
        c = 1 - self.c if dc else self.c
        return self.at(x, y, z, c)


def remote(src, dst, ssem, rsem, device):
    return pltpu.make_async_remote_copy(
        src_ref=src, dst_ref=dst, send_sem=ssem, recv_sem=rsem,
        device_id=device, device_id_type=MESH,
    )


def ring4(me, axis, block, half, ssem, rsem, late):
    at = me.x if axis == "dx" else me.y

    def copy(k):
        if k < 2:
            ref = block(at)
        else:
            ref = half(wrap(at - 1 if k == 2 else at + 1, 4), k - 2)
        to = me.off(**{axis: 1 if k in (0, 2) else -1})
        return remote(ref, ref, ssem.at[k], rsem.at[k], to)

    def arrived(k):
        if k == 0:
            ref = block(wrap(at - 1, 4))
        elif k == 1:
            ref = block(wrap(at + 1, 4))
        else:
            ref = half(wrap(at + 2, 4), k - 2)
        return remote(ref, ref, ssem.at[k], rsem.at[k], me.off(**{axis: 1}))

    copy(0).start()
    copy(1).start()
    yield
    arrived(0).wait_recv()
    copy(2).start()
    arrived(1).wait_recv()
    copy(3).start()
    yield
    arrived(2).wait_recv()
    arrived(3).wait_recv()
    for k in range(4):
        late.append(functools.partial(copy, k))


def ring8(me, block, half, ssem, rsem, late):
    z = me.z

    def copy(d, k):
        origin = wrap(z - k, NZ) if d == 0 else wrap(z + k, NZ)
        ref = block(origin) if k < 3 else half(origin, d)
        return remote(ref, ref, ssem.at[d, k], rsem.at[d, k], me.off(dz=1 - 2 * d))

    def arrived(d, k):
        origin = wrap(z - 1 - k, NZ) if d == 0 else wrap(z + 1 + k, NZ)
        ref = block(origin) if k < 3 else half(origin, d)
        return remote(ref, ref, ssem.at[d, k], rsem.at[d, k], me.off(dz=1 - 2 * d))

    copy(0, 0).start()
    copy(1, 0).start()
    for k in range(1, 4):
        yield
        for d in range(2):
            arrived(d, k - 1).wait_recv()
            copy(d, k).start()
    yield
    for d in range(2):
        arrived(d, 3).wait_recv()
    for k in range(4):
        for d in range(2):
            late.append(functools.partial(copy, d, k))


def only(flag, steps):
    going = True
    while going:
        box = []

        @pl.when(flag)
        def _():
            box.append(next(steps, "end"))

        going = box[0] != "end"
        if going:
            yield


def spread_y(me, block, half, ssem, rsem, late):
    up, down = me.off(dy=1), me.off(dy=-1)
    yh = me.yh

    def pair(ref, k, to):
        return remote(ref, ref, ssem.at[k], rsem.at[k], to)

    @pl.when(me.decode)
    def _():
        pair(block(yh), 0, up).start()
        pair(block(yh), 1, down).start()

    yield

    @pl.when(me.prefill)
    def _():
        pair(block(1 - yh), 0, up).wait_recv()
        pair(half(1 - yh, 0), 2, up).start()
        pair(block(yh), 1, up).wait_recv()
        pair(half(yh, 1), 3, down).start()

    yield

    @pl.when(me.decode)
    def _():
        pair(half(1 - yh, 0), 2, up).wait_recv()
        pair(half(1 - yh, 1), 3, up).wait_recv()
        pair(block(yh), 0, up).wait_send()
        pair(block(yh), 1, down).wait_send()

    @pl.when(me.prefill)
    def _():
        pair(half(1 - yh, 0), 2, up).wait_send()
        pair(half(yh, 1), 3, down).wait_send()


def kernel(
    hid, again, q, lens, owners, fgain, kvw_h, cache_h, wout_h, vocab_h,
    lay, ent,
    kvw, cache, wv, vv, kvbuf, qs, m1, l1, o1, abuf, psend, precv, xs, xr, own, hpart,
    ga, gb, gc, acc, ssq, st1, st2, mine,
    lsem, csem, kvs_sem, kvr_sem, wsem, hs_sem, hr_sem, as_sem, ar_sem, ps_sem, xs_sem, xr_sem,
    p4s, p4r, p8s, p8r, pys, pyr, ls_sem, lr_sem, t1s, t1r, t2s, t2r, es_sem,
):
    me = Place()
    decode, prefill = me.decode, me.prefill
    x, y, z, c, yh, h, r = me.x, me.y, me.z, me.c, me.yh, me.h, me.r
    d_model = hid.shape[1]
    late = []

    cache_copies = [
        pltpu.make_async_copy(
            cache_h.at[pl.ds(i * 4, 4)], cache.at[pl.ds(i * 4, 4)], csem.at[i]
        )
        for i in range(CACHE_PARTS)
    ]
    step = d_model // KV_PARTS
    kv_copies = [
        pltpu.make_async_copy(
            kvw_h.at[pl.ds(i * step, step)], kvw.at[pl.ds(i * step, step)], lsem.at[i]
        )
        for i in range(KV_PARTS)
    ]
    w_copy = pltpu.make_async_copy(wout_h, wv.at[yh], lsem.at[KV_PARTS])
    v_copy = pltpu.make_async_copy(vocab_h, vv.at[0], lsem.at[KV_PARTS + 1])

    @pl.when(decode)
    def _():
        for cp in cache_copies:
            cp.start()

    for cp in kv_copies:
        cp.start()
    w_copy.start()
    v_copy.start()

    peers = [dict(dz=k) for k in range(1, NZ)]
    peers += [dict(dy=2, dz=k) for k in range(1, NZ)]
    peers += [dict(dx=i, dy=j) for i in range(NX) for j in range(NY) if i or j]
    peers += [dict(dc=1)]
    barrier = pltpu.get_barrier_semaphore()
    for p in peers:
        pl.semaphore_signal(barrier, 1, device_id=me.off(**p), device_id_type=MESH)
    pl.semaphore_wait(barrier, len(peers))

    vocab_swap = remote(vocab_h, vv.at[1], wsem.at[0], wsem.at[1], me.off(dc=1))
    vocab_swap.start()
    near = wrap(jnp.where(decode, y + 1, y - 1), NY)
    w_swap = remote(wout_h, wv.at[yh], wsem.at[2], wsem.at[3], me.at(x, near, z, c))
    w_swap.start()
    w_swapped = remote(wout_h, wv.at[1 - yh], wsem.at[2], wsem.at[3], me.at(x, near, z, c))

    def hidden_part(to):
        return hid.at[:, pl.ds(pl.multiple_of(to * COLS, COLS), COLS)]

    @pl.when(z == h)
    def _():
        for k in range(1, NZ):
            to = wrap(z + k, NZ)
            remote(hidden_part(to), hpart, hs_sem.at[k], hr_sem, me.at(x, y, to, c)).start()
        hpart[...] = hid[:, pl.ds(pl.multiple_of(z * COLS, COLS), COLS)]

    for g in range(8):
        qs[pl.ds(g, TOK, stride=8), :] = q[:, g * 128:(g + 1) * 128].astype(F32)
    scale = 1.0 / math.sqrt(128)

    @pl.when(prefill)
    def _():
        m1[...] = jnp.full_like(m1, NEG)
        l1[...] = jnp.zeros_like(l1)
        o1[...] = jnp.zeros_like(o1)

    @pl.when(decode)
    def _():
        cache_len = cache.shape[1]

        def rows(first):
            parts = []
            for j in range(4):
                i = first + j
                qi = qs[pl.ds(pl.multiple_of(i * 8, 8), 8), :].astype(BF)
                s = dot_t(qi, cache[i, :, 0:128]) * scale
                at = lax.broadcasted_iota(jnp.int32, (8, cache_len), 1)
                parts.append(jnp.where(at < lens[i], s, NEG))
            s = jnp.concatenate(parts, axis=0)
            top = jnp.max(s, axis=1, keepdims=True)
            p = jnp.exp(s - top)
            total = jnp.sum(p, axis=1, keepdims=True)
            pb = p.astype(BF)
            where = pl.ds(pl.multiple_of(first * 8, 32), 32)
            m1[where, :] = jnp.broadcast_to(top, (32, 128))
            l1[where, :] = jnp.broadcast_to(total, (32, 128))
            out = [dot(pb[8 * j:8 * j + 8], cache[first + j, :, 128:256]) for j in range(4)]
            o1[where, :] = jnp.concatenate(out, axis=0)

        for i in range(CACHE_PARTS):
            cache_copies[i].wait()
            rows(i * 4)

    def square(i, total):
        w = hid[:, pl.ds(pl.multiple_of(i * 1024, 1024), 1024)].astype(F32)
        return total + jnp.sum(w * w, axis=1, keepdims=True)

    total = lax.fori_loop(0, d_model // 1024, square, jnp.zeros((TOK, 1), F32))
    inv = lax.rsqrt(total / d_model + EPS)
    fresh = jnp.zeros((TOK, 256), F32)
    for i in range(KV_PARTS):
        kv_copies[i].wait()

        def part(j, sum_, i=i):
            at = pl.ds(pl.multiple_of(i * step + j * 512, 512), 512)
            n = (hid[:, at].astype(F32) * inv * again[:, at]).astype(BF)
            return sum_ + dot(n, kvw[at, :])

        fresh = lax.fori_loop(0, step // 512, part, fresh)
    fresh = fresh.astype(BF)

    up, down = me.off(dy=1), me.off(dy=-1)

    def kv_block(zz, hh):
        return kvbuf.at[zz * 2 + hh]

    @pl.when(prefill)
    def _():
        kvbuf[r] = fresh
        sent = []
        order = [(0, 1)] + [(k, j) for k in (1, 7, 2, 6, 3, 5, 4) for j in (0, 1)]
        for n, (k, j) in enumerate(order):
            cp = remote(kvbuf.at[r], kvbuf.at[r], kvs_sem.at[n], kvr_sem.at[r],
                        me.off(dz=k, dy=2 * j))
            cp.start()
            sent.append(cp)
        n = 15
        for k in (0, 1, 7, 2, 6, 3, 5, 4):
            zz = wrap(z + k, NZ)
            ref, sem = kv_block(zz, yh), kvr_sem.at[zz * 2 + yh]
            if k:
                remote(ref, ref, kvs_sem.at[n], sem, up).wait_recv()
            for to in (up, down):
                cp = remote(ref, ref, kvs_sem.at[n], sem, to)
                cp.start()
                sent.append(cp)
                n += 1
        for k in range(NZ):
            zz = wrap(z + k, NZ)
            ref, sem = kv_block(zz, 1 - yh), kvr_sem.at[zz * 2 + 1 - yh]
            remote(ref, ref, kvs_sem.at[0], sem, up).wait_recv()
        for cp in sent:
            cp.wait_send()

    @pl.when(decode)
    def _():
        for i in range(16):
            remote(kvbuf.at[i], kvbuf.at[i], kvs_sem.at[0], kvr_sem.at[i], up).wait_recv()

    keys = kvbuf[:, :, 0:128].reshape(16 * TOK, 128)
    vals = kvbuf[:, :, 128:256].reshape(16 * TOK, 128)
    own_key = fresh[:, 0:128].astype(F32)
    own_val = fresh[:, 128:256].astype(F32)
    slot = c_slot(z)
    flag = jnp.where(decode, 1, 0)
    for half in range(2):
        heads = range(half * 4, half * 4 + 4)
        qh = jnp.concatenate([q[:, g * 128:(g + 1) * 128] for g in heads], axis=0)
        s = dot_t(qh, keys) * scale
        row = r * TOK + lax.rem(lax.broadcasted_iota(jnp.int32, s.shape, 0), TOK)
        tok = lax.broadcasted_iota(jnp.int32, s.shape, 1)
        off = flag * jnp.abs(owners[...] - row) + (1 - flag) * jnp.maximum(tok - row, 0)
        s = jnp.where(off == 0, s, NEG)
        mc = jnp.concatenate([m1[pl.ds(g, TOK, stride=8), :] for g in heads], axis=0)
        lc = jnp.concatenate([l1[pl.ds(g, TOK, stride=8), :] for g in heads], axis=0)
        oc = jnp.concatenate([o1[pl.ds(g, TOK, stride=8), :] for g in heads], axis=0)
        ok = jnp.concatenate([own_key] * 4, axis=0)
        ov = jnp.concatenate([own_val] * 4, axis=0)
        so = jnp.sum(qh.astype(F32) * ok, axis=1, keepdims=True) * scale
        so = jnp.where(jnp.broadcast_to(flag, so.shape) == 1, so, NEG)
        mc, lc = mc[:, 0:1], lc[:, 0:1]
        top = jnp.maximum(jnp.maximum(jnp.max(s, axis=1, keepdims=True), mc), so)
        p = jnp.exp(s - top)
        fac = jnp.exp(mc - top)
        po = jnp.exp(so - top)
        total = jnp.sum(p, axis=1, keepdims=True) + lc * fac + po
        out = dot(p.astype(BF), vals) + oc * fac + po.astype(BF).astype(F32) * ov
        out = (out / total).astype(BF)
        for j, g in enumerate(heads):
            abuf[slot, :, g * 128:(g + 1) * 128] = out[j * TOK:(j + 1) * TOK]

    drain(ring8(
        me,
        lambda zz: abuf.at[c_slot(zz)],
        lambda zz, k: abuf.at[c_slot(zz), pl.ds(k * 16, 16)],
        as_sem, ar_sem, late,
    ))

    w_copy.wait()
    w_swapped.wait_recv()
    half_cols = COLS // 2

    def project(parity):
        rows = abuf[pl.ds(parity * 4, 4)].reshape(4 * TOK, COLS)
        return [dot(rows, wv[j]) for j in range(2)]

    for j, v in enumerate(project(1 - c)):
        psend[:, :, j * half_cols:(j + 1) * half_cols] = v.astype(BF).reshape(4, TOK, half_cols)
    swap = remote(psend, precv, ps_sem.at[0], ps_sem.at[1], me.off(dc=1))
    swap.start()
    mine_sum = project(c)
    swap.wait_recv()
    total = []
    for j in range(2):
        v = mine_sum[j].reshape(4, TOK, half_cols)
        v = v + precv[:, :, j * half_cols:(j + 1) * half_cols].astype(F32)
        xs[:, :, j * half_cols:(j + 1) * half_cols] = v.astype(BF)
        for i in range(4):
            @pl.when(x == i)
            def _(v=v, i=i, j=j):
                own[:, j * half_cols:(j + 1) * half_cols] = v[i]

    sends = []
    for k in (1, 3, 2):
        to = wrap(x + k, NX)
        cp = remote(xs.at[to], xr.at[k - 1], xs_sem.at[k - 1], xr_sem.at[k - 1], me.at(to, y, z, c))
        cp.start()
        sends.append(cp)

    @pl.when(z != h)
    def _():
        remote(hpart, hpart, hs_sem.at[0], hr_sem, up).wait_recv()

    for cp in sends:
        cp.wait_recv()
    rows_out = own[...] + hpart[...].astype(F32)
    for k in range(3):
        rows_out = rows_out + xr[k].astype(F32)
    mine[...] = rows_out.astype(BF)
    col0 = pl.multiple_of(z * COLS, COLS)

    @pl.when(decode)
    def _():
        ga[z, yh, x] = mine[0:16, 0:half_cols]
        gc[yh, z, x] = mine[0:16, half_cols:COLS]
        gb[x, yh, z] = mine[16:32, :]

    def columns_of(zz):
        return lay.at[:, pl.ds(pl.multiple_of(zz * COLS, COLS), COLS)]

    home = me.at(x, y, h, c)

    @pl.when(prefill & (z != h))
    def _():
        remote(mine, columns_of(z), ls_sem.at[0], lr_sem.at[z], home).start()

    def part_a():
        yield from only(decode, ring4(
            me, "dx", lambda i: ga.at[z, yh, i], lambda i, k: ga.at[z, yh, i, :, pl.ds(k * 256, 256)],
            p4s.at[0], p4r.at[0], late_decode))
        yield from spread_y(
            me, lambda i: ga.at[z, i], lambda i, k: ga.at[z, i, pl.ds(2 * k, 2)],
            pys.at[0], pyr.at[0], late)
        yield from ring8(
            me, lambda i: ga.at[i], lambda i, k: ga.at[i, k], p8s.at[0], p8r.at[0], late)

    def part_c():
        yield from only(decode, ring4(
            me, "dx", lambda i: gc.at[yh, z, i], lambda i, k: gc.at[yh, z, i, :, pl.ds(k * 256, 256)],
            p4s.at[1], p4r.at[1], late_decode))
        yield from only(decode, ring8(
            me, lambda i: gc.at[yh, i], lambda i, k: gc.at[yh, i, pl.ds(2 * k, 2)],
            p8s.at[1], p8r.at[1], late_decode))
        yield from spread_y(
            me, lambda i: gc.at[i], lambda i, k: gc.at[i, pl.ds(4 * k, 4)],
            pys.at[1], pyr.at[1], late)

    def part_b():
        yield from only(decode, ring8(
            me, lambda i: gb.at[x, yh, i], lambda i, k: gb.at[x, yh, i, :, pl.ds(k * 512, 512)],
            p8s.at[2], p8r.at[2], late_decode))
        yield from spread_y(
            me, lambda i: gb.at[x, i], lambda i, k: gb.at[x, i, pl.ds(4 * k, 4)],
            pys.at[2], pyr.at[2], late)
        yield from ring4(
            me, "dx", lambda i: gb.at[i], lambda i, k: gb.at[i, k], p4s.at[2], p4r.at[2], late)

    late_decode = []
    drain(part_b(), part_a(), part_c())

    holder = c == lax.rem(z, 2)
    xz = lax.div(z, 2)
    source = holder & (x == xz)

    @pl.when(decode & holder)
    def _():
        for zz in range(NZ):
            lay[0:16, zz * COLS:zz * COLS + half_cols] = ga[zz, yh, xz]
            lay[0:16, zz * COLS + half_cols:(zz + 1) * COLS] = gc[yh, zz, xz]
            lay[16:32, zz * COLS:(zz + 1) * COLS] = gb[xz, yh, zz]

    @pl.when(prefill & source)
    def _():
        for k in range(1, NZ):
            zz = wrap(z + k, NZ)
            remote(mine, columns_of(zz), ls_sem.at[0], lr_sem.at[zz], home).wait_recv()
        lay[:, pl.ds(col0, COLS)] = mine[...]
        for k in (1, 3, 2):
            remote(lay, lay, ls_sem.at[k], lr_sem.at[NZ], me.off(dx=k)).start()

    @pl.when(prefill & holder & (x != xz))
    def _():
        remote(lay, lay, ls_sem.at[1], lr_sem.at[NZ], up).wait_recv()

    core_copy = remote(lay, lay, ls_sem.at[4], lr_sem.at[NZ + 1], me.off(dc=1))

    @pl.when(holder)
    def _():
        core_copy.start()

    v_copy.wait()
    vocab_swap.wait_recv()
    acc[...] = jnp.zeros_like(acc)
    ssq[...] = jnp.zeros_like(ssq)

    def block(zz, carry):
        base = pl.multiple_of(zz * COLS, COLS)
        for j in range(2):
            lo = (ga[zz] if j == 0 else gc[:, zz]).reshape(128, half_cols)
            hi = gb[:, :, zz, :, j * half_cols:(j + 1) * half_cols].reshape(128, half_cols)
            rows = jnp.concatenate([lo, hi], axis=0).astype(F32)
            at = pl.ds(base + j * half_cols, half_cols)
            sq = rows * rows
            ssq[...] += sq[:, 0:128] + sq[:, 128:256] + sq[:, 256:384] + sq[:, 384:512]
            gained = (rows * fgain[:, at]).astype(BF)
            for k in range(2):
                acc[:, k * 256:(k + 1) * 256] += dot(gained, vv[k, at, :])
        return carry

    lax.fori_loop(0, NZ, block, 0)
    inv = lax.rsqrt(jnp.sum(ssq[...], axis=1, keepdims=True) / d_model + EPS)
    logits = acc[...] * inv
    top = jnp.max(logits, axis=1, keepdims=True)
    shifted = logits - top
    e = jnp.exp(shifted)
    mass = jnp.sum(e, axis=1, keepdims=True)
    moment = jnp.sum(e * shifted, axis=1, keepdims=True)
    lane = lax.broadcasted_iota(jnp.int32, (256, 128), 1)
    packed = jnp.where(lane == 0, top, jnp.where(lane == 1, mass, moment))
    here = x * NY + y
    st1[here] = jnp.transpose(packed)[0:8]

    def merge(ref, n):
        tops = [ref[i, 0:1, :] for i in range(n)]
        best = tops[0]
        for t in tops[1:]:
            best = jnp.maximum(best, t)
        mass = jnp.zeros_like(best)
        moment = jnp.zeros_like(best)
        for i in range(n):
            gap = tops[i] - best
            f = jnp.exp(gap)
            mass = mass + f * ref[i, 1:2, :]
            moment = moment + f * (ref[i, 2:3, :] + gap * ref[i, 1:2, :])
        return best, mass, moment

    sent = []
    for i in range(NX):
        for j in range(NY):
            n = i * NY + j
            if n:
                cp = remote(st1.at[here], st1.at[here], t1s.at[n], t1r.at[here], me.off(dx=i, dy=j))
                cp.start()
                sent.append(cp)
    for i in range(NX):
        for j in range(NY):
            if i or j:
                n = wrap(x + i, NX) * NY + wrap(y + j, NY)
                remote(st1.at[n], st1.at[n], t1s.at[0], t1r.at[n], up).wait_recv()
    best, mass, moment = merge(st1, 16)
    st2[z, 0:1, :] = best
    st2[z, 1:2, :] = mass
    st2[z, 2:3, :] = moment
    sent2 = []
    for k in (4, 3, 5, 2, 6, 1, 7):
        cp = remote(st2.at[z], st2.at[z], t2s.at[k], t2r.at[z], me.off(dz=k))
        cp.start()
        sent2.append(cp)
    for k in range(1, NZ):
        n = wrap(z + k, NZ)
        remote(st2.at[n], st2.at[n], t2s.at[0], t2r.at[n], up).wait_recv()
    best, mass, moment = merge(st2, 8)
    ent[c] = jnp.broadcast_to(jnp.log(mass) - moment / mass, (8, 256))
    final = remote(ent.at[c], ent.at[c], es_sem.at[0], es_sem.at[1], me.off(dc=1))
    final.start()
    remote(ent.at[1 - c], ent.at[1 - c], es_sem.at[0], es_sem.at[1], me.off(dc=1)).wait_recv()

    @pl.when(jnp.logical_not(holder))
    def _():
        core_copy.wait_recv()

    @pl.when(holder)
    def _():
        core_copy.wait_send()

    @pl.when(prefill & source)
    def _():
        for k in (1, 3, 2):
            remote(lay, lay, ls_sem.at[k], lr_sem.at[NZ], me.off(dx=k)).wait_send()

    @pl.when(prefill & (z != h))
    def _():
        remote(mine, columns_of(z), ls_sem.at[0], lr_sem.at[z], home).wait_send()

    @pl.when(z == h)
    def _():
        for k in range(1, NZ):
            to = wrap(z + k, NZ)
            remote(hidden_part(to), hpart, hs_sem.at[k], hr_sem, me.at(x, y, to, c)).wait_send()

    @pl.when(decode)
    def _():
        for make in late_decode:
            make().wait_send()

    for make in late:
        make().wait_send()
    for cp in sends + sent + sent2 + [final, swap, w_swap, vocab_swap]:
        cp.wait_send()


def c_slot(zz):
    return lax.rem(zz, 2) * 4 + lax.div(zz, 2)


def drain(*steps):
    live = list(steps)
    while live:
        live = [s for s in live if next(s, "end") != "end"]


def body(hidden, attn_gain, kv_weight, queries, cache_kv, lengths, block_owner, out_weight,
         final_gain, vocab_weight):
    d_model = hidden.shape[2]
    owners = jnp.repeat(block_owner, BLK)[None, :]
    vmem = pl.BlockSpec(memory_space=pltpu.VMEM)
    smem = pl.BlockSpec(memory_space=pltpu.SMEM)
    hbm = pl.BlockSpec(memory_space=pl.ANY)
    dma = pltpu.SemaphoreType.DMA
    lay, ent = pl.pallas_call(
        kernel,
        out_shape=(
            jax.ShapeDtypeStruct((TOK, d_model), BF),
            jax.ShapeDtypeStruct((2, 8, 256), F32),
        ),
        in_specs=[vmem, vmem, vmem, smem, vmem, vmem, hbm, hbm, hbm, hbm],
        out_specs=(vmem, vmem),
        scratch_shapes=[
            pltpu.VMEM(kv_weight.shape, BF),
            pltpu.VMEM(cache_kv.shape, BF),
            pltpu.VMEM((2,) + out_weight.shape, BF),
            pltpu.VMEM((2,) + vocab_weight.shape, BF),
            pltpu.VMEM((16, TOK, 256), BF),
            pltpu.VMEM((256, 128), F32),
            pltpu.VMEM((256, 128), F32),
            pltpu.VMEM((256, 128), F32),
            pltpu.VMEM((256, 128), F32),
            pltpu.VMEM((NZ, TOK, COLS), BF),
            pltpu.VMEM((4, TOK, COLS), BF),
            pltpu.VMEM((4, TOK, COLS), BF),
            pltpu.VMEM((4, TOK, COLS), BF),
            pltpu.VMEM((3, TOK, COLS), BF),
            pltpu.VMEM((TOK, COLS), F32),
            pltpu.VMEM((TOK, COLS), BF),
            pltpu.VMEM((NZ, 2, NX, 16, 512), BF),
            pltpu.VMEM((NX, 2, NZ, 16, 1024), BF),
            pltpu.VMEM((2, NZ, NX, 16, 512), BF),
            pltpu.VMEM((256, 512), F32),
            pltpu.VMEM((256, 128), F32),
            pltpu.VMEM((16, 8, 256), F32),
            pltpu.VMEM((8, 8, 256), F32),
            pltpu.VMEM((TOK, COLS), BF),
            dma((KV_PARTS + 2,)),
            dma((CACHE_PARTS,)),
            dma((31,)),
            dma((16,)),
            dma((4,)),
            dma((NZ,)),
            dma,
            dma((2, 4)),
            dma((2, 4)),
            dma((2,)),
            dma((3,)),
            dma((3,)),
            dma((3, 4)),
            dma((3, 4)),
            dma((3, 2, 4)),
            dma((3, 2, 4)),
            dma((3, 4)),
            dma((3, 4)),
            dma((5,)),
            dma((NZ + 2,)),
            dma((16,)),
            dma((16,)),
            dma((NZ,)),
            dma((NZ,)),
            dma((2,)),
        ],
        compiler_params=pltpu.CompilerParams(
            collective_id=0, has_side_effects=True, vmem_limit_bytes=56 * 1024 * 1024
        ),
        cost_estimate=pl.CostEstimate(
            flops=4_000_000_000, bytes_accessed=24_000_000, transcendentals=1_000_000
        ),
        name="step",
    )(hidden[0], attn_gain[None, :], queries[0], lengths, owners, final_gain[None, :],
      kv_weight, cache_kv, out_weight, vocab_weight)
    ent = ent[:, 0]
    low = ent[:, 0:128].reshape(2, 2, NX, 16).transpose(2, 0, 1, 3)
    high = ent[:, 128:256].reshape(2, NX, 2, 16).transpose(1, 0, 2, 3)
    entropy = jnp.concatenate([low, high], axis=3).reshape(512)
    return (lay[None], entropy)


def solution(mesh):
    return jax.shard_map(
        body,
        mesh=mesh,
        in_specs=(
            P("section", "row", None),
            P(),
            P(None, "head"),
            P("section", "row", "head"),
            P("row", None, "head"),
            P("row"),
            P(),
            P("head", "row"),
            P(),
            P(None, ("section", "head", "row")),
        ),
        out_specs=(P("section", "row", None), P()),
        check_vma=False,
    )
```

time: 766 us -> 138 us (0.18)
  waiting for transfers between devices: 518 us -> 0 us
  blocking collectives: 189 us -> 0 us
  Pallas kernels: 0 us -> 133 us
  matrix products: 13.9 us -> 0 us
  starting transfers between devices: 13.5 us -> 0 us
  between operations: 13.9 us -> 0.65 us
  other arithmetic: 10.2 us -> 0.08 us
    psum x2 -> x0, waiting for transfers between devices: 272 us -> none  [the longest x1 207 us: from_root(): return lax.psum(jnp.where(mine, array, jnp.zeros_like(array)), axis)]
    all_gather x2 -> x0, waiting for transfers between devices: 220 us -> none  [the longest x1 135 us: body(): every_row = lax.all_gather(final_rows, 'row', axis=0, tiled=True)]
    pallas_call x0 -> x1, Pallas kernels: none -> 133 us  [body(): pl.pallas_call(kernel, out_shape=(jax.ShapeDtypeStruct((TOK, d_model), BF...]
    pmax x1 -> x0, blocking collectives: 77.4 us -> none  [body(): top_logit = lax.pmax(local_top, ('section', 'head', 'row'))]
    psum x1 -> x0, blocking collectives: 73.2 us -> none  [body(): lax.psum((jnp.sum(exponent_terms, axis=1), jnp.sum(exponent_terms * shift...]
    all_gather x1 -> x0, blocking collectives: 38.1 us -> none  [body(): prompt_all = lax.all_gather(prompt_here, 'row', axis=0, tiled=True)]
    all_to_all x1 -> x0, waiting for transfers between devices: 24.7 us -> none  [body(): lax.all_to_all(summed, 'row', split_axis=0, concat_axis=1, tiled=True)]
    dot_general x6 -> x0, matrix products: 13.9 us -> none  [the longest x1 6.96 us: body(): jnp.dot(every_row, vocab_weight, preferred_element_type=jnp.float32)]
  transfers between devices with their start and end apart: 6 -> 0, of which waited for: 5 -> 0; matrix products, arithmetic and copies ran while one was open for 1% -> 0% of each run, Pallas kernels for 0% -> 0%
where the time goes in v1:
time: 138 us
  Pallas kernels  133 us (96%)
  local copies, waits for them, and re-layouts  4.88 us (4%)
    pallas_call x1, Pallas kernels, body(): pl.pallas_call(kernel, out_shape=(jax.ShapeDtypeStruct((TOK, d_model), BF...  133 us

profile of v1, /device:TPU:1, one launch (start us, length us, event | category | flops | bytes accessed | tf_op | source)
XLA Modules:
  0.0 138.2 jit_solution(7379041001628133340)
XLA Ops:
  0.6 0.7 broadcast_in_dim.13
  1.4 0.7 broadcast_in_dim_reshape.3.owners
  2.1 132.6 %step.1 = (bf16[32,8192]{1,0:T(8,128)(2,1)}, f32[2,8,256]{2,1,0:T(8,128)}) custom-call(bf16[32,8192]{1,0:T(8,128)(2,1)} %bitcast.14, f32[1,8192]{1,0:T(1,128)} %bitcast.17, bf16[32,1024]{1,0:T(8,128)(2,1)} %bitcast.16, s32[32]{0:T(128)} %lens.1, s32[1,512]{1,0:T(1,128)} %broadcast_in_dim_reshape.3.owners, f32[1,8192]{1,0:T(1,128)} %bitcast.18, ...), custom_call_target="tpu_custom_call" | custom-call | flops 4000000000 | bytes 24000000 | tf_op jit(solution)/shard_map/step/pallas_call | solution.py:625
  134.7 0.7 slice.9
  135.4 0.1 reshape.14
  135.5 0.1 reshape.13
  135.6 0.1 pad_maximum_fusion
  135.7 0.7 reshape.15
  136.4 1.9 %copy.23 = bf16[1,32,8192]{2,1,0:T(8,128)(2,1)} copy(bf16[1,32,8192]{2,1,0:T(8,128)(2,1)} %bitcast.15) | data formatting | bytes 1048576
  (4 shorter events, 0.0 us)

commit v2 on v1

v2 whole, which is shorter than its diff:
```python
import functools
import math

import jax
import jax.numpy as jnp
from jax import lax
from jax.experimental import pallas as pl
from jax.experimental.pallas import tpu as pltpu
from jax.sharding import PartitionSpec as P

MESH = pl.DeviceIdType.MESH
BF = jnp.bfloat16
F32 = jnp.float32
EPS = 1e-05
NEG = -1e30
BLK = 4
NX, NY, NZ = 4, 4, 8
TOK = 32
COLS = 1024
CACHE_PARTS = 8
KV_PARTS = 4
HALF = 512
PARTS = (("zyx", 256, 640), ("zxy", 640, 1024), ("xyz", 0, 256))


def dot(a, b):
    return jnp.dot(a, b, preferred_element_type=F32)


def dot_t(a, b):
    return lax.dot_general(a, b, (((1,), (1,)), ((), ())), preferred_element_type=F32)


def wrap(value, n):
    return lax.rem(value + n, n)


class Place:
    def __init__(self):
        s, h, r = (lax.axis_index(a) for a in ("section", "head", "row"))
        self.s, self.h, self.r = s, h, r
        self.x, self.c = lax.div(h, 2), lax.rem(h, 2)
        self.z, self.yh = lax.div(r, 2), lax.rem(r, 2)
        self.y = self.yh * 2 + s
        self.decode = s == 1
        self.prefill = s == 0

    def at(self, x, y, z, c):
        return (lax.rem(y, 2), x * 2 + c, z * 2 + lax.div(y, 2))

    def on(self, axis):
        return {"dx": (self.x, NX), "dy": (self.y, NY), "dz": (self.z, NZ)}[axis]

    def off(self, dx=0, dy=0, dz=0, dc=0):
        x = wrap(self.x + dx, NX) if dx else self.x
        y = wrap(self.y + dy, NY) if dy else self.y
        z = wrap(self.z + dz, NZ) if dz else self.z
        c = 1 - self.c if dc else self.c
        return self.at(x, y, z, c)


def remote(src, dst, ssem, rsem, device):
    return pltpu.make_async_remote_copy(
        src_ref=src, dst_ref=dst, send_sem=ssem, recv_sem=rsem,
        device_id=device, device_id_type=MESH,
    )


def unicast(me, axis, block, ssem, rsem, late):
    at, n = me.on(axis)

    def copy(k):
        ref = block(at)
        return remote(ref, ref, ssem.at[k], rsem.at[at], me.off(**{axis: k}))

    order = [k for d in range(n // 2, 0, -1) for k in sorted({d, n - d})]
    for k in order:
        copy(k).start()
        late.append(functools.partial(copy, k))
    yield
    for k in reversed(order):
        source = wrap(at + k, n)
        ref = block(source)
        remote(ref, ref, ssem.at[0], rsem.at[source], me.off(**{axis: 1})).wait_recv()


def ring4(me, axis, half, ssem, rsem, late):
    at, n = me.on(axis)

    def copy(d, k):
        ref = half(at, d if k == 0 else 1 - d) if k < 2 else half(wrap(at - 1 + 2 * d, n), d)
        return remote(ref, ref, ssem.at[d, k], rsem.at[d, k], me.off(**{axis: 1 - 2 * d}))

    def arrived(d, k):
        near = wrap(at - 1 + 2 * d, n)
        ref = half(near, d if k == 0 else 1 - d) if k < 2 else half(wrap(at + 2, n), d)
        return remote(ref, ref, ssem.at[d, k], rsem.at[d, k], me.off(**{axis: 1}))

    for k in range(2):
        for d in range(2):
            copy(d, k).start()
    yield
    for d in range(2):
        arrived(d, 0).wait_recv()
        copy(d, 2).start()
    yield
    for k in (1, 2):
        for d in range(2):
            arrived(d, k).wait_recv()
    for k in range(3):
        for d in range(2):
            late.append(functools.partial(copy, d, k))


def ring8(me, block, half, ssem, rsem, late, seen=None):
    z = me.z

    def copy(d, k):
        origin = wrap(z - k, NZ) if d == 0 else wrap(z + k, NZ)
        ref = block(origin) if k < 3 else half(origin, d)
        return remote(ref, ref, ssem.at[d, k], rsem.at[d, k], me.off(dz=1 - 2 * d))

    def arrived(d, k):
        origin = wrap(z - 1 - k, NZ) if d == 0 else wrap(z + 1 + k, NZ)
        ref = block(origin) if k < 3 else half(origin, d)
        return remote(ref, ref, ssem.at[d, k], rsem.at[d, k], me.off(dz=1))

    copy(0, 0).start()
    copy(1, 0).start()
    if seen:
        seen(0)
    for k in range(1, 4):
        yield
        for d in range(2):
            arrived(d, k - 1).wait_recv()
            copy(d, k).start()
            if seen:
                seen(k if d else -k)
    yield
    for d in range(2):
        arrived(d, 3).wait_recv()
    if seen:
        seen(4)
    for k in range(4):
        for d in range(2):
            late.append(functools.partial(copy, d, k))


def kernel(
    hid, again, q, lens, block_owner, fgain, kvw_h, cache_h, wout_h, vocab_h,
    lay, ent,
    kvw, cache, wv, vv, kvbuf, qs, m1, l1, o1, abuf, psend, precv, xs, xr, own, hpart, fin,
    b0, b1, b2, acc, ssq, st1, st2, ends,
    lsem, csem, kvs_sem, kvr_sem, vsem, hs_sem, hr_sem, as_sem, ar_sem, ays_sem, ayr_sem,
    ps_sem, xs_sem, xr_sem,
    uni_s, uni_r, p4s, p4r, p8s, p8r, ls_sem, lr_sem, core_sem, t1s, t1r, t2s, t2r, es_sem,
):
    me = Place()
    decode, prefill = me.decode, me.prefill
    x, y, z, c, yh, h, r = me.x, me.y, me.z, me.c, me.yh, me.h, me.r
    d_model = hid.shape[1]
    late = []
    near = wrap(jnp.where(decode, y + 1, y - 1), NY)
    home_y = jnp.where(decode, near, y)
    holder = c == lax.rem(z, 2)
    xz = lax.div(z, 2)

    cache_copies = [
        pltpu.make_async_copy(
            cache_h.at[pl.ds(i * 4, 4)], cache.at[pl.ds(i * 4, 4)], csem.at[i]
        )
        for i in range(CACHE_PARTS)
    ]
    step = d_model // KV_PARTS
    kv_copies = [
        pltpu.make_async_copy(
            kvw_h.at[pl.ds(i * step, step)], kvw.at[pl.ds(i * step, step)], lsem.at[i]
        )
        for i in range(KV_PARTS)
    ]
    w_copy = pltpu.make_async_copy(wout_h, wv, lsem.at[KV_PARTS])
    v_copy = pltpu.make_async_copy(vocab_h, vv.at[0], lsem.at[KV_PARTS + 1])
    for cp in kv_copies:
        cp.start()

    @pl.when(decode)
    def _():
        for cp in cache_copies:
            cp.start()

    w_copy.start()
    v_copy.start()

    peers = [dict(dz=k) for k in range(1, NZ)]
    peers += [dict(dy=2, dz=k) for k in range(1, NZ)]
    peers += [dict(dx=i, dy=j) for i in range(NX) for j in range(NY) if i or j]
    peers += [dict(dc=1)]
    barrier = pltpu.get_barrier_semaphore()
    for p in peers:
        pl.semaphore_signal(barrier, 1, device_id=me.off(**p), device_id_type=MESH)
    for k in range(1, NZ):
        to = me.at(x, near, wrap(z + k, NZ), c)
        pl.semaphore_signal(barrier, 1, device_id=to, device_id_type=MESH)

    @pl.when(prefill & holder)
    def _():
        for k in range(NZ):
            zz = wrap(z + k, NZ)
            pl.semaphore_signal(barrier, 1, device_id=me.at(xz, near, zz, c), device_id_type=MESH)
            if k:
                pl.semaphore_signal(barrier, 1, device_id=me.at(xz, y, zz, c), device_id_type=MESH)

        @pl.when(x != xz)
        def _():
            pl.semaphore_signal(barrier, 1, device_id=me.at(xz, y, z, c), device_id_type=MESH)

    def square(i, total):
        w = hid[:, pl.ds(pl.multiple_of(i * 1024, 1024), 1024)].astype(F32)
        return total + jnp.sum(w * w, axis=1, keepdims=True)

    total = lax.fori_loop(0, d_model // 1024, square, jnp.zeros((TOK, 1), F32))
    inv = lax.rsqrt(total / d_model + EPS)
    fresh = jnp.zeros((TOK, 256), F32)
    for i in range(KV_PARTS):
        kv_copies[i].wait()

        def part(j, sum_, i=i):
            at = pl.ds(pl.multiple_of(i * step + j * 512, 512), 512)
            n = (hid[:, at].astype(F32) * inv * again[:, at]).astype(BF)
            return sum_ + dot(n, kvw[at, :])

        fresh = lax.fori_loop(0, step // 512, part, fresh)
    fresh = fresh.astype(BF)

    for g in range(8):
        qs[pl.ds(g, TOK, stride=8), :] = q[:, g * 128:(g + 1) * 128].astype(F32)
    scale = 1.0 / math.sqrt(128)

    at_home = prefill & (z == h)
    extra = jnp.where(at_home, 3, 4)
    pl.semaphore_wait(barrier, len(peers) + NZ - 1 + extra)

    vocab_swap = remote(vocab_h, vv.at[1], vsem.at[0], vsem.at[1], me.off(dc=1))

    def hidden_part(zz, half):
        return pl.ds(pl.multiple_of(zz * COLS + half * HALF, HALF), HALF)

    def hidden_copy(k, other):
        zz = wrap(z + k, NZ)
        src = hid.at[:, hidden_part(zz, 1 - yh if other else yh)]
        to = me.at(x, near if other else y, zz, c)
        return remote(src, hpart.at[other], hs_sem.at[k, other], hr_sem.at[other], to)

    def send_later_needs():
        vocab_swap.start()

        @pl.when(z == h)
        def _():
            for k in range(NZ):
                if k:
                    hidden_copy(k, 0).start()
                hidden_copy(k, 1).start()
            hpart[0] = hid[:, hidden_part(z, yh)]

    up, down = me.off(dy=1), me.off(dy=-1)

    @pl.when(prefill)
    def _():
        m1[...] = jnp.full_like(m1, NEG)
        l1[...] = jnp.zeros_like(l1)
        o1[...] = jnp.zeros_like(o1)
        kvbuf[r] = fresh
        sent = []
        order = [(0, 1)] + [(k, j) for k in (1, 7, 2, 6, 3, 5, 4) for j in (0, 1)]
        for n, (k, j) in enumerate(order):
            cp = remote(kvbuf.at[r], kvbuf.at[r], kvs_sem.at[n], kvr_sem.at[r],
                        me.off(dz=k, dy=2 * j))
            cp.start()
            sent.append(cp)
        n = 15
        for k in (0, 1, 7, 2, 6, 3, 5, 4):
            i = wrap(z + k, NZ) * 2 + yh
            ref, sem = kvbuf.at[i], kvr_sem.at[i]
            if k:
                remote(ref, ref, kvs_sem.at[n], sem, up).wait_recv()
            for to in (up, down):
                cp = remote(ref, ref, kvs_sem.at[n], sem, to)
                cp.start()
                sent.append(cp)
                n += 1
        send_later_needs()
        for k in range(NZ):
            i = wrap(z + k, NZ) * 2 + 1 - yh
            remote(kvbuf.at[i], kvbuf.at[i], kvs_sem.at[0], kvr_sem.at[i], up).wait_recv()
        for cp in sent:
            cp.wait_send()

    @pl.when(decode)
    def _():
        send_later_needs()
        cache_len = cache.shape[1]

        def rows(first):
            parts = []
            for j in range(4):
                i = first + j
                qi = qs[pl.ds(pl.multiple_of(i * 8, 8), 8), :].astype(BF)
                s = dot_t(qi, cache[i, :, 0:128]) * scale
                at = lax.broadcasted_iota(jnp.int32, (8, cache_len), 1)
                parts.append(jnp.where(at < lens[i], s, NEG))
            s = jnp.concatenate(parts, axis=0)
            top = jnp.max(s, axis=1, keepdims=True)
            p = jnp.exp(s - top)
            total = jnp.sum(p, axis=1, keepdims=True)
            pb = p.astype(BF)
            where = pl.ds(pl.multiple_of(first * 8, 32), 32)
            m1[where, :] = jnp.broadcast_to(top, (32, 128))
            l1[where, :] = jnp.broadcast_to(total, (32, 128))
            out = [dot(pb[8 * j:8 * j + 8], cache[first + j, :, 128:256]) for j in range(4)]
            o1[where, :] = jnp.concatenate(out, axis=0)

        for i in range(CACHE_PARTS):
            cache_copies[i].wait()
            rows(i * 4)
        for i in range(16):
            remote(kvbuf.at[i], kvbuf.at[i], kvs_sem.at[0], kvr_sem.at[i], up).wait_recv()

    keys = kvbuf[:, :, 0:128].reshape(16 * TOK, 128)
    vals = kvbuf[:, :, 128:256].reshape(16 * TOK, 128)
    own_key = fresh[:, 0:128].astype(F32)
    own_val = fresh[:, 128:256].astype(F32)
    flag = jnp.where(decode, 1, 0)
    n_block = block_owner.shape[1]
    digits = jnp.broadcast_to(block_owner[...], (8, n_block))
    spread = lax.broadcasted_iota(jnp.int32, (n_block, n_block * BLK), 1) // BLK
    spread = spread == lax.broadcasted_iota(jnp.int32, (n_block, n_block * BLK), 0)
    spread = spread.astype(F32).astype(BF)
    high = dot((digits >> 4).astype(F32).astype(BF), spread)
    low = dot((digits & 15).astype(F32).astype(BF), spread)
    owners = (high[0:1] * 16.0 + low[0:1]).astype(jnp.int32)

    def a_block(zz, plane):
        return abuf.at[lax.rem(zz, 2), lax.div(zz, 2), plane]

    for half in range(2):
        heads = range(half * 4, half * 4 + 4)
        qh = jnp.concatenate([q[:, g * 128:(g + 1) * 128] for g in heads], axis=0)
        s = dot_t(qh, keys) * scale
        row = r * TOK + lax.rem(lax.broadcasted_iota(jnp.int32, s.shape, 0), TOK)
        tok = lax.broadcasted_iota(jnp.int32, s.shape, 1)
        off = flag * jnp.abs(owners - row) + (1 - flag) * jnp.maximum(tok - row, 0)
        s = jnp.where(off == 0, s, NEG)
        mc = jnp.concatenate([m1[pl.ds(g, TOK, stride=8), :] for g in heads], axis=0)
        lc = jnp.concatenate([l1[pl.ds(g, TOK, stride=8), :] for g in heads], axis=0)
        oc = jnp.concatenate([o1[pl.ds(g, TOK, stride=8), :] for g in heads], axis=0)
        ok = jnp.concatenate([own_key] * 4, axis=0)
        ov = jnp.concatenate([own_val] * 4, axis=0)
        so = jnp.sum(qh.astype(F32) * ok, axis=1, keepdims=True) * scale
        so = jnp.where(jnp.broadcast_to(flag, so.shape) == 1, so, NEG)
        mc, lc = mc[:, 0:1], lc[:, 0:1]
        top = jnp.maximum(jnp.maximum(jnp.max(s, axis=1, keepdims=True), mc), so)
        p = jnp.exp(s - top)
        fac = jnp.exp(mc - top)
        po = jnp.exp(so - top)
        total = jnp.sum(p, axis=1, keepdims=True) + lc * fac + po
        out = dot(p.astype(BF), vals) + oc * fac + po.astype(BF).astype(F32) * ov
        out = (out / total).astype(BF)
        for j, g in enumerate(heads):
            a_block(z, 0)[:, g * 128:(g + 1) * 128] = out[j * TOK:(j + 1) * TOK]

    def share(k):
        zz = wrap(z + k, NZ)
        to = me.at(x, near, z, c)
        return remote(a_block(zz, 0), a_block(zz, 1), ays_sem.at[k % NZ], ayr_sem.at[zz], to)

    drain(ring8(
        me,
        lambda zz: a_block(zz, 0),
        lambda zz, k: a_block(zz, 0).at[pl.ds(k * 16, 16)],
        as_sem, ar_sem, late, seen=lambda k: share(k).start(),
    ))
    w_copy.wait()
    for k in (0, 1, -1, 2, -2, 3, -3, 4):
        share(k).wait_recv()

    def project(parity):
        return dot(abuf[parity].reshape(8 * TOK, COLS), wv[...]).reshape(NX, 2, TOK, HALF)

    psend[...] = project(1 - c).astype(BF)
    swap = remote(psend, precv, ps_sem.at[0], ps_sem.at[1], me.off(dc=1))
    swap.start()
    total = project(c)
    swap.wait_recv()
    total = total + precv[...].astype(F32)
    xs[...] = total.astype(BF)
    sends = []
    for k in (2, 1, 3):
        to = wrap(x + k, NX)
        cp = remote(xs.at[to], xr.at[k - 1], xs_sem.at[k - 1], xr_sem.at[k - 1], me.at(to, y, z, c))
        cp.start()
        sends.append(cp)
    for i in range(NX):
        @pl.when(x == i)
        def _(i=i):
            own[...] = total[i]

    @pl.when(z != h)
    def _():
        hidden_copy(0, 0).wait_recv()

    hidden_copy(0, 1).wait_recv()
    rows_out = own[...] + hpart[...].astype(F32)
    for cp in sends:
        cp.wait_recv()
    for k in range(3):
        rows_out = rows_out + xr[k].astype(F32)
    fin[...] = rows_out.astype(BF)

    rows_d = fin[1 - me.s]
    strip = jnp.concatenate([rows_d[0:16], rows_d[16:32]], axis=1)
    spot = {"x": x, "y": y, "z": z}
    bufs = (b0, b1, b2)
    for (order, lo, hi), buf in zip(PARTS, bufs):
        buf[tuple(spot[a] for a in reversed(order))] = strip[:, lo:hi]

    def way(p):
        order, lo, hi = PARTS[p]
        buf = bufs[p]
        a1, a2, a3 = order
        i2, i3 = spot[a2], spot[a3]
        n1, n2 = buf.shape[2], buf.shape[1]
        yield from unicast(me, "d" + a1, lambda i: buf.at[i3, i2, i], uni_s.at[p], uni_r.at[p], late)
        yield from ring4(
            me, "d" + a2, lambda i, k: buf.at[i3, i, pl.ds(k * (n1 // 2), n1 // 2)],
            p4s.at[p, 0], p4r.at[p, 0], late)
        if a3 == "z":
            yield from ring8(
                me, lambda i: buf.at[i], lambda i, k: buf.at[i, pl.ds(k * (n2 // 2), n2 // 2)],
                p8s, p8r, late)
        else:
            yield from ring4(
                me, "d" + a3, lambda i, k: buf.at[i, pl.ds(k * (n2 // 2), n2 // 2)],
                p4s.at[p, 1], p4r.at[p, 1], late)

    def owner_cols(zz, half):
        return lay.at[:, pl.ds(pl.multiple_of(zz * COLS + half * HALF, HALF), HALF)]

    def owner_copy(k):
        n = z * 2 + yh
        to = me.at(wrap(x + k, NX), home_y, h, c)
        return remote(fin.at[me.s], owner_cols(z, yh), ls_sem.at[k], lr_sem.at[n], to)

    core_copy = remote(lay, lay, core_sem.at[0], core_sem.at[1], me.off(dc=1))

    def prefill_rows():
        for k in (2, 1, 3):
            owner_copy(k).start()

        @pl.when(jnp.logical_not(at_home))
        def _():
            owner_copy(0).start()

        @pl.when(at_home)
        def _():
            owner_cols(z, yh)[...] = fin[0]

        yield
        yield
        yield

        @pl.when(prefill & holder)
        def _():
            for k in range(NZ):
                zz = wrap(z + k, NZ)
                for half in (yh, 1 - yh):
                    def wait(zz=zz, half=half):
                        ref = owner_cols(zz, half)
                        remote(ref, ref, ls_sem.at[0], lr_sem.at[zz * 2 + half], up).wait_recv()
                    if k == 0 and half is yh:
                        pl.when(x != xz)(wait)
                    else:
                        wait()
            core_copy.start()

    drain(*([way(p) for p in range(len(PARTS))] + [prefill_rows()]))

    def held(i_x, i_y, i_z):
        at = {"x": i_x, "y": i_y, "z": i_z}
        pieces = {}
        for (order, lo, hi), buf in zip(PARTS, bufs):
            pieces[lo] = buf[tuple(at[a] for a in reversed(order))]
        line = jnp.concatenate([pieces[lo] for lo in sorted(pieces)], axis=1)
        return line[:, 0:HALF], line[:, HALF:COLS]

    @pl.when(decode & holder)
    def _():
        for zz in range(NZ):
            for half in range(2):
                i_y = jnp.where(yh == half, 2 * yh + 1, 2 * half)
                low, high = held(xz, i_y, zz)
                at = zz * COLS + half * HALF
                lay[0:16, at:at + HALF] = low
                lay[16:32, at:at + HALF] = high
        core_copy.start()

    v_copy.wait()
    vocab_swap.wait_recv()
    acc[...] = jnp.zeros_like(acc)
    ssq[...] = jnp.zeros_like(ssq)

    def block(zz, carry):
        base = pl.multiple_of(zz * COLS, COLS)
        for half in range(2):
            rows = []
            for i_x in range(NX):
                for plane in range(2):
                    rows += held(i_x, 2 * plane + 1 if half == plane else 2 * half, zz)
            rows = jnp.concatenate(rows, axis=0).astype(F32)
            at = pl.ds(base + half * HALF, HALF)
            sq = rows * rows
            ssq[...] += sq[:, 0:128] + sq[:, 128:256] + sq[:, 256:384] + sq[:, 384:512]
            gained = (rows * fgain[:, at]).astype(BF)
            for k in range(2):
                acc[:, k * 256:(k + 1) * 256] += dot(gained, vv[k, at, :])
        return carry

    lax.fori_loop(0, NZ, block, 0)
    inv = lax.rsqrt(jnp.sum(ssq[...], axis=1, keepdims=True) / d_model + EPS)
    logits = acc[...] * inv
    top = jnp.max(logits, axis=1, keepdims=True)
    shifted = logits - top
    e = jnp.exp(shifted)
    mass = jnp.sum(e, axis=1, keepdims=True)
    moment = jnp.sum(e * shifted, axis=1, keepdims=True)
    lane = lax.broadcasted_iota(jnp.int32, (256, 128), 1)
    packed = jnp.where(lane == 0, top, jnp.where(lane == 1, mass, moment))
    here = x * NY + y
    st1[here] = jnp.transpose(packed)[0:8]

    def merge(ref, n):
        tops = [ref[i, 0:1, :] for i in range(n)]
        best = tops[0]
        for t in tops[1:]:
            best = jnp.maximum(best, t)
        mass = jnp.zeros_like(best)
        moment = jnp.zeros_like(best)
        for i in range(n):
            gap = tops[i] - best
            f = jnp.exp(gap)
            mass = mass + f * ref[i, 1:2, :]
            moment = moment + f * (ref[i, 2:3, :] + gap * ref[i, 1:2, :])
        return best, mass, moment

    sent = []
    for i in range(NX):
        for j in range(NY):
            n = i * NY + j
            if n:
                cp = remote(st1.at[here], st1.at[here], t1s.at[n], t1r.at[here], me.off(dx=i, dy=j))
                cp.start()
                sent.append(cp)
    for i in range(NX):
        for j in range(NY):
            if i or j:
                n = wrap(x + i, NX) * NY + wrap(y + j, NY)
                remote(st1.at[n], st1.at[n], t1s.at[0], t1r.at[n], up).wait_recv()
    best, mass, moment = merge(st1, 16)
    st2[z, 0:1, :] = best
    st2[z, 1:2, :] = mass
    st2[z, 2:3, :] = moment
    sent2 = []
    for k in (4, 3, 5, 2, 6, 1, 7):
        cp = remote(st2.at[z], st2.at[z], t2s.at[k], t2r.at[z], me.off(dz=k))
        cp.start()
        sent2.append(cp)
    for k in range(1, NZ):
        n = wrap(z + k, NZ)
        remote(st2.at[n], st2.at[n], t2s.at[0], t2r.at[n], up).wait_recv()
    best, mass, moment = merge(st2, 8)
    ends[c] = jnp.broadcast_to(jnp.log(mass) - moment / mass, (8, 256))
    final = remote(ends.at[c], ends.at[c], es_sem.at[0], es_sem.at[1], me.off(dc=1))
    final.start()
    remote(ends.at[1 - c], ends.at[1 - c], es_sem.at[0], es_sem.at[1], me.off(dc=1)).wait_recv()
    for i in range(NX):
        ent[i:i + 1, :] = jnp.concatenate(
            [ends[k, 0:1, i * 64:(i + 1) * 64] for k in range(2)], axis=1)

    @pl.when(jnp.logical_not(holder))
    def _():
        core_copy.wait_recv()

    @pl.when(holder)
    def _():
        core_copy.wait_send()

    for k in (1, 2, 3):
        owner_copy(k).wait_send()

    @pl.when(jnp.logical_not(at_home))
    def _():
        owner_copy(0).wait_send()

    @pl.when(z == h)
    def _():
        for k in range(NZ):
            if k:
                hidden_copy(k, 0).wait_send()
            hidden_copy(k, 1).wait_send()

    for k in range(NZ):
        share(k).wait_send()
    for make in late:
        make().wait_send()
    for cp in sends + sent + sent2 + [final, swap, vocab_swap]:
        cp.wait_send()


def drain(*steps):
    live = list(steps)
    while live:
        live = [s for s in live if next(s, "end") != "end"]


def body(hidden, attn_gain, kv_weight, queries, cache_kv, lengths, block_owner, out_weight,
         final_gain, vocab_weight):
    d_model = hidden.shape[2]
    vmem = pl.BlockSpec(memory_space=pltpu.VMEM)
    smem = pl.BlockSpec(memory_space=pltpu.SMEM)
    hbm = pl.BlockSpec(memory_space=pl.ANY)
    dma = pltpu.SemaphoreType.DMA
    size = {"x": NX, "y": NY, "z": NZ}
    spread = [
        pltpu.VMEM(tuple(size[a] for a in reversed(order)) + (16, hi - lo), BF)
        for order, lo, hi in PARTS
    ]
    n = len(PARTS)
    lay, ent = pl.pallas_call(
        kernel,
        out_shape=(
            jax.ShapeDtypeStruct((TOK, d_model), BF),
            jax.ShapeDtypeStruct((NX, 128), F32),
        ),
        in_specs=[vmem, vmem, vmem, smem, vmem, vmem, hbm, hbm, hbm, hbm],
        out_specs=(vmem, vmem),
        scratch_shapes=[
            pltpu.VMEM(kv_weight.shape, BF),
            pltpu.VMEM(cache_kv.shape, BF),
            pltpu.VMEM(out_weight.shape, BF),
            pltpu.VMEM((2,) + vocab_weight.shape, BF),
            pltpu.VMEM((16, TOK, 256), BF),
            pltpu.VMEM((256, 128), F32),
            pltpu.VMEM((256, 128), F32),
            pltpu.VMEM((256, 128), F32),
            pltpu.VMEM((256, 128), F32),
            pltpu.VMEM((2, NX, 2, TOK, COLS), BF),
            pltpu.VMEM((NX, 2, TOK, HALF), BF),
            pltpu.VMEM((NX, 2, TOK, HALF), BF),
            pltpu.VMEM((NX, 2, TOK, HALF), BF),
            pltpu.VMEM((3, 2, TOK, HALF), BF),
            pltpu.VMEM((2, TOK, HALF), F32),
            pltpu.VMEM((2, TOK, HALF), BF),
            pltpu.VMEM((2, TOK, HALF), BF),
            *spread,
            pltpu.VMEM((256, 512), F32),
            pltpu.VMEM((256, 128), F32),
            pltpu.VMEM((16, 8, 256), F32),
            pltpu.VMEM((8, 8, 256), F32),
            pltpu.VMEM((2, 8, 256), F32),
            dma((KV_PARTS + 2,)),
            dma((CACHE_PARTS,)),
            dma((31,)),
            dma((16,)),
            dma((2,)),
            dma((NZ, 2)),
            dma((2,)),
            dma((2, 4)),
            dma((2, 4)),
            dma((NZ,)),
            dma((NZ,)),
            dma((2,)),
            dma((3,)),
            dma((3,)),
            dma((n, NZ)),
            dma((n, NZ)),
            dma((n, 2, 2, 3)),
            dma((n, 2, 2, 3)),
            dma((2, 4)),
            dma((2, 4)),
            dma((4,)),
            dma((16,)),
            dma((2,)),
            dma((16,)),
            dma((16,)),
            dma((NZ,)),
            dma((NZ,)),
            dma((2,)),
        ],
        compiler_params=pltpu.CompilerParams(
            collective_id=0, has_side_effects=True, vmem_limit_bytes=56 * 1024 * 1024
        ),
        cost_estimate=pl.CostEstimate(
            flops=4_000_000_000, bytes_accessed=24_000_000, transcendentals=1_000_000
        ),
        name="step",
    )(hidden[0], attn_gain[None, :], queries[0], lengths, block_owner[None, :], final_gain[None, :],
      kv_weight, cache_kv, out_weight, vocab_weight)
    return (lay[None], ent.reshape(512))


def solution(mesh):
    return jax.shard_map(
        body,
        mesh=mesh,
        in_specs=(
            P("section", "row", None),
            P(),
            P(None, "head"),
            P("section", "row", "head"),
            P("row", None, "head"),
            P("row"),
            P(),
            P("head", "row"),
            P(),
            P(None, ("section", "head", "row")),
        ),
        out_specs=(P("section", "row", None), P()),
        check_vma=False,
    )
```

time: 138 us -> 113 us (0.82)
  Pallas kernels: 133 us -> 109 us
  local copies, waits for them, and re-layouts: 4.88 us -> 3.12 us
    pallas_call x1, Pallas kernels: 133 us -> 109 us  [body(): pl.pallas_call(kernel, out_shape=(jax.ShapeDtypeStruct((TOK, d_model), BF...]
where the time goes in v2:
time: 113 us
  Pallas kernels  109 us (96%)
  local copies, waits for them, and re-layouts  3.12 us (3%)
    pallas_call x1, Pallas kernels, body(): pl.pallas_call(kernel, out_shape=(jax.ShapeDtypeStruct((TOK, d_model), BF...  109 us
    unnamed x2, local copies, waits for them, and re-layouts  3.12 us

profile of v2, /device:TPU:1, one launch (start us, length us, event | category | flops | bytes accessed | tf_op | source)
XLA Modules:
  0.0 113.0 jit_solution(1050529692332684883)
XLA Ops:
  0.6 109.2 %step.1 = (bf16[32,8192]{1,0:T(8,128)(2,1)}, f32[4,128]{1,0:T(4,128)}) custom-call(bf16[32,8192]{1,0:T(8,128)(2,1)} %bitcast.7, f32[1,8192]{1,0:T(1,128)} %bitcast.10, bf16[32,1024]{1,0:T(8,128)(2,1)} %bitcast.9, s32[32]{0:T(128)} %lens.1, s32[1,128]{1,0:T(1,128)} %bitcast.13, f32[1,8192]{1,0:T(1,128)} %bitcast.11, bf16[8192,256]{1,0:T(8,128)(2,1)} %kvw_h.1, ...), custom_call_target="tpu_custom_call" | custom-call | flops 4000000000 | bytes 24000000 | tf_op jit(solution)/shard_map/step/pallas_call | solution.py:637
  109.9 1.9 %copy.14 = bf16[1,32,8192]{2,1,0:T(8,128)(2,1)} copy(bf16[1,32,8192]{2,1,0:T(8,128)(2,1)} %bitcast.8) | data formatting | bytes 1048576
  111.7 1.3 %copy.15 = f32[512]{0:T(512)} copy(f32[512]{0:T(512)} %bitcast.12) | data formatting | bytes 4096

commit v3 on v2

--- a/solution.py
+++ b/solution.py
@@ -20,7 +20,7 @@
 CACHE_PARTS = 8
 KV_PARTS = 4
 HALF = 512
-PARTS = (("zyx", 256, 640), ("zxy", 640, 1024), ("xyz", 0, 256))
+PARTS = (("xyz", 0, 256), ("zyx", 256, 640), ("zxy", 640, 1024))
 
 
 def dot(a, b):
@@ -103,7 +103,7 @@
     for d in range(2):
         arrived(d, 0).wait_recv()
         copy(d, 2).start()
-    yield
+    yield "tail"
     for k in (1, 2):
         for d in range(2):
             arrived(d, k).wait_recv()
@@ -136,7 +136,7 @@
             copy(d, k).start()
             if seen:
                 seen(k if d else -k)
-    yield
+    yield "tail"
     for d in range(2):
         arrived(d, 3).wait_recv()
     if seen:
@@ -148,13 +148,17 @@
 
 def kernel(
     hid, again, q, lens, block_owner, fgain, kvw_h, cache_h, wout_h, vocab_h,
-    lay, ent,
-    kvw, cache, wv, vv, kvbuf, qs, m1, l1, o1, abuf, psend, precv, xs, xr, own, hpart, fin,
-    b0, b1, b2, acc, ssq, st1, st2, ends,
-    lsem, csem, kvs_sem, kvr_sem, vsem, hs_sem, hr_sem, as_sem, ar_sem, ays_sem, ayr_sem,
-    ps_sem, xs_sem, xr_sem,
-    uni_s, uni_r, p4s, p4r, p8s, p8r, ls_sem, lr_sem, core_sem, t1s, t1r, t2s, t2r, es_sem,
+    lay_out, ent,
+    lay, kvw, cache, wv, vv, kvbuf, qs, m1, l1, o1, abuf, psend, precv, xs, xr, own, hpart, fin,
+    *rest,
 ):
+    bufs = rest[:len(PARTS)]
+    (
+        acc, ssq, st1, st2,
+        lsem, csem, kvs_sem, kvr_sem, vsem, hs_sem, hr_sem, as_sem, ar_sem, ays_sem, ayr_sem, fs_sem, fr_sem,
+        ps_sem, xs_sem, xr_sem,
+        uni_s, uni_r, p4s, p4r, p8s, p8r, ls_sem, lr_sem, core_sem, t1s, t1r, t2s, t2r, es_sem,
+    ) = rest[len(PARTS):]
     me = Place()
     decode, prefill = me.decode, me.prefill
     x, y, z, c, yh, h, r = me.x, me.y, me.z, me.c, me.yh, me.h, me.r
@@ -191,10 +195,14 @@
     w_copy.start()
     v_copy.start()
 
+    @pl.when(prefill)
+    def _():
+        kvbuf[...] = jnp.zeros_like(kvbuf)
+
     peers = [dict(dz=k) for k in range(1, NZ)]
     peers += [dict(dy=2, dz=k) for k in range(1, NZ)]
     peers += [dict(dx=i, dy=j) for i in range(NX) for j in range(NY) if i or j]
-    peers += [dict(dc=1)]
+    peers += [dict(dc=1, dz=k) for k in range(NZ)]
     barrier = pltpu.get_barrier_semaphore()
     for p in peers:
         pl.semaphore_signal(barrier, 1, device_id=me.off(**p), device_id_type=MESH)
@@ -271,13 +279,22 @@
         o1[...] = jnp.zeros_like(o1)
         kvbuf[r] = fresh
         sent = []
-        order = [(0, 1)] + [(k, j) for k in (1, 7, 2, 6, 3, 5, 4) for j in (0, 1)]
-        for n, (k, j) in enumerate(order):
-            cp = remote(kvbuf.at[r], kvbuf.at[r], kvs_sem.at[n], kvr_sem.at[r],
-                        me.off(dz=k, dy=2 * j))
+        for n, k in enumerate((1, 7, 2, 6, 3, 5, 4)):
+            cp = remote(kvbuf.at[r], kvbuf.at[r], kvs_sem.at[n], kvr_sem.at[r], me.off(dz=k))
             cp.start()
             sent.append(cp)
-        n = 15
+
+        def across(k):
+            return remote(kvbuf.at[r], kvbuf.at[r], kvs_sem.at[23 + k], kvr_sem.at[r],
+                          me.off(dz=k, dy=2))
+
+        across(0).start()
+        for k in range(1, NZ):
+            @pl.when(z + k < NZ)
+            def _(k=k):
+                across(k).start()
+
+        n = 7
         for k in (0, 1, 7, 2, 6, 3, 5, 4):
             i = wrap(z + k, NZ) * 2 + yh
             ref, sem = kvbuf.at[i], kvr_sem.at[i]
@@ -290,10 +307,18 @@
                 n += 1
         send_later_needs()
         for k in range(NZ):
-            i = wrap(z + k, NZ) * 2 + 1 - yh
-            remote(kvbuf.at[i], kvbuf.at[i], kvs_sem.at[0], kvr_sem.at[i], up).wait_recv()
+            @pl.when(k <= z)
+            def _(k=k):
+                i = k * 2 + 1 - yh
+                remote(kvbuf.at[i], kvbuf.at[i], kvs_sem.at[0], kvr_sem.at[i], up).wait_recv()
+
         for cp in sent:
             cp.wait_send()
+        across(0).wait_send()
+        for k in range(1, NZ):
+            @pl.when(z + k < NZ)
+            def _(k=k):
+                across(k).wait_send()
 
     @pl.when(decode)
     def _():
@@ -339,8 +364,44 @@
     low = dot((digits & 15).astype(F32).astype(BF), spread)
     owners = (high[0:1] * 16.0 + low[0:1]).astype(jnp.int32)
 
-    def a_block(zz, plane):
-        return abuf.at[lax.rem(zz, 2), lax.div(zz, 2), plane]
+    def a_block(zz, plane, part):
+        return abuf.at[lax.rem(zz, 2), part, lax.div(zz, 2), plane]
+
+    def share(k, part):
+        zz = wrap(z + k, NZ)
+        to = me.at(x, near, z, c)
+        return remote(a_block(zz, 0, part), a_block(zz, 1, part),
+                      ays_sem.at[part, k % NZ], ayr_sem.at[part, zz], to)
+
+    def share_far(d, part):
+        zz = wrap(z - 3 + 6 * d, NZ)
+        to = me.at(x, near, wrap(z + 1 - 2 * d, NZ), c)
+        rows = pl.ds(d * 16, 16)
+        return remote(a_block(zz, 0, part).at[rows], a_block(zz, 1, part).at[rows],
+                      fs_sem.at[part, d], fr_sem.at[part, d], to)
+
+    def shared_far(d, part):
+        zz = wrap(z + 4, NZ)
+        rows = pl.ds(d * 16, 16)
+        return remote(a_block(zz, 0, part).at[rows], a_block(zz, 1, part).at[rows],
+                      fs_sem.at[part, d], fr_sem.at[part, d], me.at(x, near, z, c))
+
+    def a_ring(part):
+        def seen(k):
+            if k == 4:
+                return
+            if abs(k) == 3:
+                share_far(0 if k < 0 else 1, part).start()
+            share(k, part).start()
+
+        return ring8(
+            me,
+            lambda zz: a_block(zz, 0, part),
+            lambda zz, k: a_block(zz, 0, part).at[pl.ds(k * 16, 16)],
+            as_sem.at[part], ar_sem.at[part], late, seen=seen,
+        )
+
+    rings = []
 
     for half in range(2):
         heads = range(half * 4, half * 4 + 4)
@@ -366,25 +427,22 @@
         out = dot(p.astype(BF), vals) + oc * fac + po.astype(BF).astype(F32) * ov
         out = (out / total).astype(BF)
         for j, g in enumerate(heads):
-            a_block(z, 0)[:, g * 128:(g + 1) * 128] = out[j * TOK:(j + 1) * TOK]
-
-    def share(k):
-        zz = wrap(z + k, NZ)
-        to = me.at(x, near, z, c)
-        return remote(a_block(zz, 0), a_block(zz, 1), ays_sem.at[k % NZ], ayr_sem.at[zz], to)
-
-    drain(ring8(
-        me,
-        lambda zz: a_block(zz, 0),
-        lambda zz, k: a_block(zz, 0).at[pl.ds(k * 16, 16)],
-        as_sem, ar_sem, late, seen=lambda k: share(k).start(),
-    ))
+            a_block(z, 0, half)[:, j * 128:(j + 1) * 128] = out[j * TOK:(j + 1) * TOK]
+        rings.append(a_ring(half))
+        next(rings[-1])
+
+    drain(*rings)
     w_copy.wait()
-    for k in (0, 1, -1, 2, -2, 3, -3, 4):
-        share(k).wait_recv()
+    for part in range(2):
+        for k in (0, 1, -1, 2, -2, 3, -3):
+            share(k, part).wait_recv()
+        for d in range(2):
+            shared_far(d, part).wait_recv()
 
     def project(parity):
-        return dot(abuf[parity].reshape(8 * TOK, COLS), wv[...]).reshape(NX, 2, TOK, HALF)
+        rows = [abuf[parity, part].reshape(8 * TOK, HALF) for part in range(2)]
+        total = dot(rows[0], wv[0:HALF, :]) + dot(rows[1], wv[HALF:COLS, :])
+        return total.reshape(NX, 2, TOK, HALF)
 
     psend[...] = project(1 - c).astype(BF)
     swap = remote(psend, precv, ps_sem.at[0], ps_sem.at[1], me.off(dc=1))
@@ -419,7 +477,6 @@
     rows_d = fin[1 - me.s]
     strip = jnp.concatenate([rows_d[0:16], rows_d[16:32]], axis=1)
     spot = {"x": x, "y": y, "z": z}
-    bufs = (b0, b1, b2)
     for (order, lo, hi), buf in zip(PARTS, bufs):
         buf[tuple(spot[a] for a in reversed(order))] = strip[:, lo:hi]
 
@@ -430,17 +487,22 @@
         i2, i3 = spot[a2], spot[a3]
         n1, n2 = buf.shape[2], buf.shape[1]
         yield from unicast(me, "d" + a1, lambda i: buf.at[i3, i2, i], uni_s.at[p], uni_r.at[p], late)
-        yield from ring4(
-            me, "d" + a2, lambda i, k: buf.at[i3, i, pl.ds(k * (n1 // 2), n1 // 2)],
-            p4s.at[p, 0], p4r.at[p, 0], late)
-        if a3 == "z":
+        if a2 == "z":
             yield from ring8(
-                me, lambda i: buf.at[i], lambda i, k: buf.at[i, pl.ds(k * (n2 // 2), n2 // 2)],
-                p8s, p8r, late)
+                me, lambda i: buf.at[i3, i],
+                lambda i, k: buf.at[i3, i, pl.ds(k * (n1 // 2), n1 // 2)], p8s.at[p], p8r.at[p], late)
         else:
             yield from ring4(
+                me, "d" + a2, lambda i, k: buf.at[i3, i, pl.ds(k * (n1 // 2), n1 // 2)],
+                p4s.at[p, 0], p4r.at[p, 0], late)
+        if a3 == "z":
+            yield from last(ring8(
+                me, lambda i: buf.at[i], lambda i, k: buf.at[i, pl.ds(k * (n2 // 2), n2 // 2)],
+                p8s.at[p], p8r.at[p], late))
+        else:
+            yield from last(ring4(
                 me, "d" + a3, lambda i, k: buf.at[i, pl.ds(k * (n2 // 2), n2 // 2)],
-                p4s.at[p, 1], p4r.at[p, 1], late)
+                p4s.at[p, 1], p4r.at[p, 1], late))
 
     def owner_cols(zz, half):
         return lay.at[:, pl.ds(pl.multiple_of(zz * COLS + half * HALF, HALF), HALF)]
@@ -452,37 +514,18 @@
 
     core_copy = remote(lay, lay, core_sem.at[0], core_sem.at[1], me.off(dc=1))
 
-    def prefill_rows():
-        for k in (2, 1, 3):
-            owner_copy(k).start()
-
-        @pl.when(jnp.logical_not(at_home))
-        def _():
-            owner_copy(0).start()
-
-        @pl.when(at_home)
-        def _():
-            owner_cols(z, yh)[...] = fin[0]
-
-        yield
-        yield
-        yield
-
-        @pl.when(prefill & holder)
-        def _():
-            for k in range(NZ):
-                zz = wrap(z + k, NZ)
-                for half in (yh, 1 - yh):
-                    def wait(zz=zz, half=half):
-                        ref = owner_cols(zz, half)
-                        remote(ref, ref, ls_sem.at[0], lr_sem.at[zz * 2 + half], up).wait_recv()
-                    if k == 0 and half is yh:
-                        pl.when(x != xz)(wait)
-                    else:
-                        wait()
-            core_copy.start()
-
-    drain(*([way(p) for p in range(len(PARTS))] + [prefill_rows()]))
+    drain(*[way(p) for p in range(len(PARTS))])
+
+    for k in (2, 1, 3):
+        owner_copy(k).start()
+
+    @pl.when(jnp.logical_not(at_home))
+    def _():
+        owner_copy(0).start()
+
+    @pl.when(at_home)
+    def _():
+        owner_cols(z, yh)[...] = fin[0]
 
     def held(i_x, i_y, i_z):
         at = {"x": i_x, "y": i_y, "z": i_z}
@@ -535,10 +578,12 @@
     lane = lax.broadcasted_iota(jnp.int32, (256, 128), 1)
     packed = jnp.where(lane == 0, top, jnp.where(lane == 1, mass, moment))
     here = x * NY + y
-    st1[here] = jnp.transpose(packed)[0:8]
+    lines = jnp.transpose(packed)
+    st1[here] = jnp.concatenate(
+        [lines[i:i + 1, j * 128:(j + 1) * 128] for i in (0, 1, 2, 2) for j in range(2)], axis=0)
 
     def merge(ref, n):
-        tops = [ref[i, 0:1, :] for i in range(n)]
+        tops = [ref[i, 0:2, :] for i in range(n)]
         best = tops[0]
         for t in tops[1:]:
             best = jnp.maximum(best, t)
@@ -547,8 +592,8 @@
         for i in range(n):
             gap = tops[i] - best
             f = jnp.exp(gap)
-            mass = mass + f * ref[i, 1:2, :]
-            moment = moment + f * (ref[i, 2:3, :] + gap * ref[i, 1:2, :])
+            mass = mass + f * ref[i, 2:4, :]
+            moment = moment + f * (ref[i, 4:6, :] + gap * ref[i, 2:4, :])
         return best, mass, moment
 
     sent = []
@@ -565,29 +610,51 @@
                 n = wrap(x + i, NX) * NY + wrap(y + j, NY)
                 remote(st1.at[n], st1.at[n], t1s.at[0], t1r.at[n], up).wait_recv()
     best, mass, moment = merge(st1, 16)
-    st2[z, 0:1, :] = best
-    st2[z, 1:2, :] = mass
-    st2[z, 2:3, :] = moment
-    sent2 = []
-    for k in (4, 3, 5, 2, 6, 1, 7):
-        cp = remote(st2.at[z], st2.at[z], t2s.at[k], t2r.at[z], me.off(dz=k))
-        cp.start()
-        sent2.append(cp)
-    for k in range(1, NZ):
-        n = wrap(z + k, NZ)
-        remote(st2.at[n], st2.at[n], t2s.at[0], t2r.at[n], up).wait_recv()
-    best, mass, moment = merge(st2, 8)
-    ends[c] = jnp.broadcast_to(jnp.log(mass) - moment / mass, (8, 256))
-    final = remote(ends.at[c], ends.at[c], es_sem.at[0], es_sem.at[1], me.off(dc=1))
-    final.start()
-    remote(ends.at[1 - c], ends.at[1 - c], es_sem.at[0], es_sem.at[1], me.off(dc=1)).wait_recv()
+    st2[c, z] = jnp.concatenate([best, mass, moment, moment], axis=0)
+
+    def totals(k, other):
+        return remote(st2.at[c, z], st2.at[c, z], t2s.at[k, other], t2r.at[c, z],
+                      me.off(dz=k, dc=other))
+
+    last_step = [(k, j) for k in (4, 3, 5, 2, 6, 1, 7, 0) for j in (0, 1) if k or j]
+    for k, j in last_step:
+        totals(k, j).start()
+
+    @pl.when(prefill & holder)
+    def _():
+        for k in range(NZ):
+            zz = wrap(z + k, NZ)
+            for half in (yh, 1 - yh):
+                def wait(zz=zz, half=half):
+                    ref = owner_cols(zz, half)
+                    remote(ref, ref, ls_sem.at[0], lr_sem.at[zz * 2 + half], up).wait_recv()
+                if k == 0 and half is yh:
+                    pl.when(x != xz)(wait)
+                else:
+                    wait()
+        core_copy.start()
+
+    @pl.when(jnp.logical_not(holder))
+    def _():
+        core_copy.wait_recv()
+
+    out_copy = pltpu.make_async_copy(lay, lay_out, es_sem)
+    out_copy.start()
+    for i in range(NZ):
+        for j in range(2):
+            at = 1 - c if j else c
+            n = wrap(z + i, NZ)
+            if i or j:
+                remote(st2.at[at, n], st2.at[at, n], t2s.at[0, 0], t2r.at[at, n], up).wait_recv()
+    sides = []
+    for j in range(2):
+        best, mass, moment = merge(st2.at[j], NZ)
+        sides.append(jnp.log(mass) - moment / mass)
     for i in range(NX):
+        at = (i % 2) * 64
         ent[i:i + 1, :] = jnp.concatenate(
-            [ends[k, 0:1, i * 64:(i + 1) * 64] for k in range(2)], axis=1)
-
-    @pl.when(jnp.logical_not(holder))
-    def _():
-        core_copy.wait_recv()
+            [side[i // 2:i // 2 + 1, at:at + 64] for side in sides], axis=1)
+    out_copy.wait()
 
     @pl.when(holder)
     def _():
@@ -607,18 +674,38 @@
                 hidden_copy(k, 0).wait_send()
             hidden_copy(k, 1).wait_send()
 
-    for k in range(NZ):
-        share(k).wait_send()
+    for part in range(2):
+        for k in (0, 1, -1, 2, -2, 3, -3):
+            share(k, part).wait_send()
+        for d in range(2):
+            share_far(d, part).wait_send()
     for make in late:
         make().wait_send()
-    for cp in sends + sent + sent2 + [final, swap, vocab_swap]:
+    for k, j in last_step:
+        totals(k, j).wait_send()
+    for cp in sends + sent + [swap, vocab_swap]:
         cp.wait_send()
 
 
 def drain(*steps):
-    live = list(steps)
+    live, ends = list(steps), []
     while live:
-        live = [s for s in live if next(s, "end") != "end"]
+        going = []
+        for s in live:
+            told = next(s, "end")
+            if told == "last":
+                ends.append(s)
+            elif told != "end":
+                going.append(s)
+        live = going
+    for s in ends:
+        for _ in s:
+            pass
+
+
+def last(steps):
+    for told in steps:
+        yield "last" if told == "tail" else told
 
 
 def body(hidden, attn_gain, kv_weight, queries, cache_kv, lengths, block_owner, out_weight,
@@ -641,8 +728,9 @@
             jax.ShapeDtypeStruct((NX, 128), F32),
         ),
         in_specs=[vmem, vmem, vmem, smem, vmem, vmem, hbm, hbm, hbm, hbm],
-        out_specs=(vmem, vmem),
+        out_specs=(hbm, vmem),
         scratch_shapes=[
+            pltpu.VMEM((TOK, d_model), BF),
             pltpu.VMEM(kv_weight.shape, BF),
             pltpu.VMEM(cache_kv.shape, BF),
             pltpu.VMEM(out_weight.shape, BF),
@@ -652,7 +740,7 @@
             pltpu.VMEM((256, 128), F32),
             pltpu.VMEM((256, 128), F32),
             pltpu.VMEM((256, 128), F32),
-            pltpu.VMEM((2, NX, 2, TOK, COLS), BF),
+            pltpu.VMEM((2, 2, NX, 2, TOK, HALF), BF),
             pltpu.VMEM((NX, 2, TOK, HALF), BF),
             pltpu.VMEM((NX, 2, TOK, HALF), BF),
             pltpu.VMEM((NX, 2, TOK, HALF), BF),
@@ -663,9 +751,8 @@
             *spread,
             pltpu.VMEM((256, 512), F32),
             pltpu.VMEM((256, 128), F32),
-            pltpu.VMEM((16, 8, 256), F32),
-            pltpu.VMEM((8, 8, 256), F32),
-            pltpu.VMEM((2, 8, 256), F32),
+            pltpu.VMEM((16, 8, 128), F32),
+            pltpu.VMEM((2, NZ, 8, 128), F32),
             dma((KV_PARTS + 2,)),
             dma((CACHE_PARTS,)),
             dma((31,)),
@@ -673,10 +760,12 @@
             dma((2,)),
             dma((NZ, 2)),
             dma((2,)),
-            dma((2, 4)),
-            dma((2, 4)),
-            dma((NZ,)),
-            dma((NZ,)),
+            dma((2, 2, 4)),
+            dma((2, 2, 4)),
+            dma((2, NZ)),
+            dma((2, NZ)),
+            dma((2, 2)),
+            dma((2, 2)),
             dma((2,)),
             dma((3,)),
             dma((3,)),
@@ -684,16 +773,16 @@
             dma((n, NZ)),
             dma((n, 2, 2, 3)),
             dma((n, 2, 2, 3)),
-            dma((2, 4)),
-            dma((2, 4)),
+            dma((n, 2, 4)),
+            dma((n, 2, 4)),
             dma((4,)),
             dma((16,)),
             dma((2,)),
             dma((16,)),
             dma((16,)),
-            dma((NZ,)),
-            dma((NZ,)),
-            dma((2,)),
+            dma((NZ, 2)),
+            dma((2, NZ)),
+            dma,
         ],
         compiler_params=pltpu.CompilerParams(
             collective_id=0, has_side_effects=True, vmem_limit_bytes=56 * 1024 * 1024

time: 113 us -> 102 us (0.903)
  Pallas kernels: 109 us -> 98.3 us
    pallas_call x1, Pallas kernels: 109 us -> 98.3 us  [body(): pl.pallas_call(kernel, out_shape=(jax.ShapeDtypeStruct((TOK, d_model), BF...]
where the time goes in v3:
time: 102 us
  Pallas kernels  98.3 us (96%)
  local copies, waits for them, and re-layouts  3.12 us (3%)
    pallas_call x1, Pallas kernels, body(): pl.pallas_call(kernel, out_shape=(jax.ShapeDtypeStruct((TOK, d_model), BF...  98.3 us
    unnamed x2, local copies, waits for them, and re-layouts  3.12 us

profile of v3, /device:TPU:1, one launch (start us, length us, event | category | flops | bytes accessed | tf_op | source)
XLA Modules:
  0.0 102.1 jit_solution(7828813480791370987)
XLA Ops:
  0.6 98.3 %step.1 = (bf16[32,8192]{1,0:T(8,128)(2,1)}, f32[4,128]{1,0:T(4,128)}) custom-call(bf16[32,8192]{1,0:T(8,128)(2,1)} %bitcast.7, f32[1,8192]{1,0:T(1,128)} %bitcast.10, bf16[32,1024]{1,0:T(8,128)(2,1)} %bitcast.9, s32[32]{0:T(128)} %lens.1, s32[1,128]{1,0:T(1,128)} %bitcast.13, f32[1,8192]{1,0:T(1,128)} %bitcast.11, bf16[8192,256]{1,0:T(8,128)(2,1)} %kvw_h.1, ...), custom_call_target="tpu_custom_call" | custom-call | flops 4000000000 | bytes 24000000 | tf_op jit(solution)/shard_map/step/pallas_call | solution.py:724
  99.0 1.9 %copy.14 = bf16[1,32,8192]{2,1,0:T(8,128)(2,1)} copy(bf16[1,32,8192]{2,1,0:T(8,128)(2,1)} %bitcast.8) | data formatting | bytes 1048576
  100.8 1.3 %copy.15 = f32[512]{0:T(512)} copy(f32[512]{0:T(512)} %bitcast.12) | data formatting | bytes 4096

commit v4 on v3

--- a/solution.py
+++ b/solution.py
@@ -20,7 +20,7 @@
 CACHE_PARTS = 8
 KV_PARTS = 4
 HALF = 512
-PARTS = (("xyz", 0, 256), ("zyx", 256, 640), ("zxy", 640, 1024))
+PARTS = (("yxz", 0, 384), ("zyx", 384, 768), ("zxy", 768, 1024))
 
 
 def dot(a, b):
@@ -112,40 +112,6 @@
             late.append(functools.partial(copy, d, k))
 
 
-def ring8(me, block, half, ssem, rsem, late, seen=None):
-    z = me.z
-
-    def copy(d, k):
-        origin = wrap(z - k, NZ) if d == 0 else wrap(z + k, NZ)
-        ref = block(origin) if k < 3 else half(origin, d)
-        return remote(ref, ref, ssem.at[d, k], rsem.at[d, k], me.off(dz=1 - 2 * d))
-
-    def arrived(d, k):
-        origin = wrap(z - 1 - k, NZ) if d == 0 else wrap(z + 1 + k, NZ)
-        ref = block(origin) if k < 3 else half(origin, d)
-        return remote(ref, ref, ssem.at[d, k], rsem.at[d, k], me.off(dz=1))
-
-    copy(0, 0).start()
-    copy(1, 0).start()
-    if seen:
-        seen(0)
-    for k in range(1, 4):
-        yield
-        for d in range(2):
-            arrived(d, k - 1).wait_recv()
-            copy(d, k).start()
-            if seen:
-                seen(k if d else -k)
-    yield "tail"
-    for d in range(2):
-        arrived(d, 3).wait_recv()
-    if seen:
-        seen(4)
-    for k in range(4):
-        for d in range(2):
-            late.append(functools.partial(copy, d, k))
-
-
 def kernel(
     hid, again, q, lens, block_owner, fgain, kvw_h, cache_h, wout_h, vocab_h,
     lay_out, ent,
@@ -157,7 +123,7 @@
         acc, ssq, st1, st2,
         lsem, csem, kvs_sem, kvr_sem, vsem, hs_sem, hr_sem, as_sem, ar_sem, ays_sem, ayr_sem, fs_sem, fr_sem,
         ps_sem, xs_sem, xr_sem,
-        uni_s, uni_r, p4s, p4r, p8s, p8r, ls_sem, lr_sem, core_sem, t1s, t1r, t2s, t2r, es_sem,
+        uni_s, uni_r, mid_s, mid_r, p4s, p4r, p8s, p8r, ls_sem, lr_sem, core_sem, t1s, t1r, t2s, t2r, es_sem,
     ) = rest[len(PARTS):]
     me = Place()
     decode, prefill = me.decode, me.prefill
@@ -373,33 +339,59 @@
         return remote(a_block(zz, 0, part), a_block(zz, 1, part),
                       ays_sem.at[part, k % NZ], ayr_sem.at[part, zz], to)
 
-    def share_far(d, part):
-        zz = wrap(z - 3 + 6 * d, NZ)
-        to = me.at(x, near, wrap(z + 1 - 2 * d, NZ), c)
-        rows = pl.ds(d * 16, 16)
-        return remote(a_block(zz, 0, part).at[rows], a_block(zz, 1, part).at[rows],
-                      fs_sem.at[part, d], fr_sem.at[part, d], to)
-
-    def shared_far(d, part):
-        zz = wrap(z + 4, NZ)
-        rows = pl.ds(d * 16, 16)
-        return remote(a_block(zz, 0, part).at[rows], a_block(zz, 1, part).at[rows],
-                      fs_sem.at[part, d], fr_sem.at[part, d], me.at(x, near, z, c))
+    def first(d, k, part):
+        ref = a_block(z, 0, part)
+        return remote(ref, ref, as_sem.at[part, d, k - 1], ar_sem.at[part, d, k - 1],
+                      me.off(dz=k * (1 - 2 * d)))
+
+    def first_came(d, k, part):
+        ref = a_block(wrap(z - k * (1 - 2 * d), NZ), 0, part)
+        return remote(ref, ref, as_sem.at[part, d, k - 1], ar_sem.at[part, d, k - 1], me.off(dz=1))
+
+    def piece(zz, plane, part, d, k):
+        ref = a_block(zz, plane, part)
+        return ref.at[pl.ds(d * 16, 16)] if k == 2 else ref
+
+    def onward(d, k, plane, part):
+        sign = 1 - 2 * d
+        zz = wrap(z - 2 * sign, NZ)
+        to = me.at(x, near if plane else y, wrap(z + k * sign, NZ), c)
+        return remote(piece(zz, 0, part, d, k), piece(zz, plane, part, d, k),
+                      fs_sem.at[part, plane, d, k - 1], fr_sem.at[part, plane, d, k - 1], to)
+
+    def onward_came(d, k, plane, part):
+        zz = wrap(z - (2 + k) * (1 - 2 * d), NZ)
+        ref = piece(zz, plane, part, d, k)
+        return remote(ref, ref, fs_sem.at[part, plane, d, k - 1],
+                      fr_sem.at[part, plane, d, k - 1], me.off(dz=1))
 
     def a_ring(part):
-        def seen(k):
-            if k == 4:
-                return
-            if abs(k) == 3:
-                share_far(0 if k < 0 else 1, part).start()
-            share(k, part).start()
-
-        return ring8(
-            me,
-            lambda zz: a_block(zz, 0, part),
-            lambda zz, k: a_block(zz, 0, part).at[pl.ds(k * 16, 16)],
-            as_sem.at[part], ar_sem.at[part], late, seen=seen,
-        )
+        def go(make, *what):
+            make(*what, part).start()
+            late.append(functools.partial(make, *what, part))
+
+        for d in range(2):
+            go(first, d, 2)
+        go(share, 0)
+        for d in range(2):
+            go(first, d, 1)
+        yield
+        for d in range(2):
+            first_came(d, 2, part).wait_recv()
+            for k, plane in ((2, 1), (2, 0), (1, 1), (1, 0)):
+                go(onward, d, k, plane)
+        yield
+        for d in range(2):
+            first_came(d, 1, part).wait_recv()
+            go(share, 2 * d - 1)
+            go(share, 4 * d - 2)
+        yield "last"
+        for plane in range(2):
+            for d in range(2):
+                for k in (1, 2):
+                    onward_came(d, k, plane, part).wait_recv()
+        for k in (0, 1, -1, 2, -2):
+            share(k, part).wait_recv()
 
     rings = []
 
@@ -433,11 +425,6 @@
 
     drain(*rings)
     w_copy.wait()
-    for part in range(2):
-        for k in (0, 1, -1, 2, -2, 3, -3):
-            share(k, part).wait_recv()
-        for d in range(2):
-            shared_far(d, part).wait_recv()
 
     def project(parity):
         rows = [abuf[parity, part].reshape(8 * TOK, HALF) for part in range(2)]
@@ -485,24 +472,17 @@
         buf = bufs[p]
         a1, a2, a3 = order
         i2, i3 = spot[a2], spot[a3]
-        n1, n2 = buf.shape[2], buf.shape[1]
+        n2 = buf.shape[1]
         yield from unicast(me, "d" + a1, lambda i: buf.at[i3, i2, i], uni_s.at[p], uni_r.at[p], late)
-        if a2 == "z":
-            yield from ring8(
-                me, lambda i: buf.at[i3, i],
-                lambda i, k: buf.at[i3, i, pl.ds(k * (n1 // 2), n1 // 2)], p8s.at[p], p8r.at[p], late)
-        else:
-            yield from ring4(
-                me, "d" + a2, lambda i, k: buf.at[i3, i, pl.ds(k * (n1 // 2), n1 // 2)],
-                p4s.at[p, 0], p4r.at[p, 0], late)
+        yield from unicast(me, "d" + a2, lambda i: buf.at[i3, i], mid_s.at[p], mid_r.at[p], late)
         if a3 == "z":
-            yield from last(ring8(
-                me, lambda i: buf.at[i], lambda i, k: buf.at[i, pl.ds(k * (n2 // 2), n2 // 2)],
+            yield from last(ring8_halves(
+                me, lambda i, k: buf.at[i, pl.ds(k * (n2 // 2), n2 // 2)],
                 p8s.at[p], p8r.at[p], late))
         else:
             yield from last(ring4(
                 me, "d" + a3, lambda i, k: buf.at[i, pl.ds(k * (n2 // 2), n2 // 2)],
-                p4s.at[p, 1], p4r.at[p, 1], late))
+                p4s.at[p], p4r.at[p], late))
 
     def owner_cols(zz, half):
         return lay.at[:, pl.ds(pl.multiple_of(zz * COLS + half * HALF, HALF), HALF)]
@@ -514,18 +494,35 @@
 
     core_copy = remote(lay, lay, core_sem.at[0], core_sem.at[1], me.off(dc=1))
 
-    drain(*[way(p) for p in range(len(PARTS))])
-
-    for k in (2, 1, 3):
-        owner_copy(k).start()
-
-    @pl.when(jnp.logical_not(at_home))
-    def _():
-        owner_copy(0).start()
-
-    @pl.when(at_home)
-    def _():
-        owner_cols(z, yh)[...] = fin[0]
+    def prefill_rows():
+        for k in (2, 1, 3):
+            owner_copy(k).start()
+
+        @pl.when(jnp.logical_not(at_home))
+        def _():
+            owner_copy(0).start()
+
+        @pl.when(at_home)
+        def _():
+            owner_cols(z, yh)[...] = fin[0]
+
+        yield
+
+    drain(*[way(p) for p in range(len(PARTS))], prefill_rows())
+
+
+    @pl.when(prefill & holder)
+    def _():
+        for k in range(NZ):
+            zz = wrap(z + k, NZ)
+            for half in (yh, 1 - yh):
+                def wait(zz=zz, half=half):
+                    ref = owner_cols(zz, half)
+                    remote(ref, ref, ls_sem.at[0], lr_sem.at[zz * 2 + half], up).wait_recv()
+                if k == 0 and half is yh:
+                    pl.when(x != xz)(wait)
+                else:
+                    wait()
 
     def held(i_x, i_y, i_z):
         at = {"x": i_x, "y": i_y, "z": i_z}
@@ -544,7 +541,13 @@
                 at = zz * COLS + half * HALF
                 lay[0:16, at:at + HALF] = low
                 lay[16:32, at:at + HALF] = high
+
+    out_copy = pltpu.make_async_copy(lay, lay_out, es_sem)
+
+    @pl.when(holder)
+    def _():
         core_copy.start()
+        out_copy.start()
 
     v_copy.wait()
     vocab_swap.wait_recv()
@@ -597,13 +600,18 @@
         return best, mass, moment
 
     sent = []
-    for i in range(NX):
-        for j in range(NY):
+    for i in (2, 1, 3, 0):
+        for j in (2, 1, 3, 0):
             n = i * NY + j
             if n:
                 cp = remote(st1.at[here], st1.at[here], t1s.at[n], t1r.at[here], me.off(dx=i, dy=j))
                 cp.start()
                 sent.append(cp)
+    @pl.when(jnp.logical_not(holder))
+    def _():
+        core_copy.wait_recv()
+        out_copy.start()
+
     for i in range(NX):
         for j in range(NY):
             if i or j:
@@ -620,26 +628,6 @@
     for k, j in last_step:
         totals(k, j).start()
 
-    @pl.when(prefill & holder)
-    def _():
-        for k in range(NZ):
-            zz = wrap(z + k, NZ)
-            for half in (yh, 1 - yh):
-                def wait(zz=zz, half=half):
-                    ref = owner_cols(zz, half)
-                    remote(ref, ref, ls_sem.at[0], lr_sem.at[zz * 2 + half], up).wait_recv()
-                if k == 0 and half is yh:
-                    pl.when(x != xz)(wait)
-                else:
-                    wait()
-        core_copy.start()
-
-    @pl.when(jnp.logical_not(holder))
-    def _():
-        core_copy.wait_recv()
-
-    out_copy = pltpu.make_async_copy(lay, lay_out, es_sem)
-    out_copy.start()
     for i in range(NZ):
         for j in range(2):
             at = 1 - c if j else c
@@ -674,17 +662,42 @@
                 hidden_copy(k, 0).wait_send()
             hidden_copy(k, 1).wait_send()
 
-    for part in range(2):
-        for k in (0, 1, -1, 2, -2, 3, -3):
-            share(k, part).wait_send()
-        for d in range(2):
-            share_far(d, part).wait_send()
     for make in late:
         make().wait_send()
     for k, j in last_step:
         totals(k, j).wait_send()
     for cp in sends + sent + [swap, vocab_swap]:
         cp.wait_send()
+
+
+def ring8_halves(me, half, ssem, rsem, late):
+    z = me.z
+
+    def copy(d, k, j):
+        ref = half(wrap(z - k, NZ) if d == 0 else wrap(z + k, NZ), d if j == 0 else 1 - d)
+        return remote(ref, ref, ssem.at[d, k, j], rsem.at[d, k, j], me.off(dz=1 - 2 * d))
+
+    def arrived(d, k, j):
+        ref = half(wrap(z - 1 - k, NZ) if d == 0 else wrap(z + 1 + k, NZ), d if j == 0 else 1 - d)
+        return remote(ref, ref, ssem.at[d, k, j], rsem.at[d, k, j], me.off(dz=1))
+
+    for j in range(2):
+        for d in range(2):
+            copy(d, 0, j).start()
+    for k in range(1, 4):
+        for j in range(2):
+            yield
+            for d in range(2):
+                arrived(d, k - 1, j).wait_recv()
+                if k < 3 or j == 0:
+                    copy(d, k, j).start()
+    yield "tail"
+    for d in range(2):
+        arrived(d, 3, 0).wait_recv()
+    for k in range(4):
+        for j in range(2 if k < 3 else 1):
+            for d in range(2):
+                late.append(functools.partial(copy, d, k, j))
 
 
 def drain(*steps):
@@ -760,21 +773,23 @@
             dma((2,)),
             dma((NZ, 2)),
             dma((2,)),
-            dma((2, 2, 4)),
-            dma((2, 2, 4)),
+            dma((2, 2, 2)),
+            dma((2, 2, 2)),
             dma((2, NZ)),
             dma((2, NZ)),
-            dma((2, 2)),
-            dma((2, 2)),
+            dma((2, 2, 2, 2)),
+            dma((2, 2, 2, 2)),
             dma((2,)),
             dma((3,)),
             dma((3,)),
             dma((n, NZ)),
             dma((n, NZ)),
-            dma((n, 2, 2, 3)),
-            dma((n, 2, 2, 3)),
-            dma((n, 2, 4)),
-            dma((n, 2, 4)),
+            dma((n, NZ)),
+            dma((n, NZ)),
+            dma((n, 2, 3)),
+            dma((n, 2, 3)),
+            dma((n, 2, 4, 2)),
+            dma((n, 2, 4, 2)),
             dma((4,)),
             dma((16,)),
             dma((2,)),

time: 102 us -> 98.9 us (0.970)
  Pallas kernels: 98.3 us -> 95 us
    pallas_call x1, Pallas kernels: 98.3 us -> 95 us  [body(): pl.pallas_call(kernel, out_shape=(jax.ShapeDtypeStruct((TOK, d_model), BF...]
where the time goes in v4:
time: 98.9 us; the launch traced here: 98.7 us
  Pallas kernels  95 us (96%)
  local copies, waits for them, and re-layouts  3.12 us (3%)
    pallas_call x1, Pallas kernels, body(): pl.pallas_call(kernel, out_shape=(jax.ShapeDtypeStruct((TOK, d_model), BF...  95 us
    unnamed x2, local copies, waits for them, and re-layouts  3.12 us

profile of v4, /device:TPU:1, one launch (start us, length us, event | category | flops | bytes accessed | tf_op | source)
XLA Modules:
  0.0 98.7 jit_solution(14522456167322911815)
XLA Ops:
  0.6 95.0 %step.1 = (bf16[32,8192]{1,0:T(8,128)(2,1)}, f32[4,128]{1,0:T(4,128)}) custom-call(bf16[32,8192]{1,0:T(8,128)(2,1)} %bitcast.7, f32[1,8192]{1,0:T(1,128)} %bitcast.10, bf16[32,1024]{1,0:T(8,128)(2,1)} %bitcast.9, s32[32]{0:T(128)} %lens.1, s32[1,128]{1,0:T(1,128)} %bitcast.13, f32[1,8192]{1,0:T(1,128)} %bitcast.11, bf16[8192,256]{1,0:T(8,128)(2,1)} %kvw_h.1, ...), custom_call_target="tpu_custom_call" | custom-call | flops 4000000000 | bytes 24000000 | tf_op jit(solution)/shard_map/step/pallas_call | solution.py:737
  95.6 1.9 %copy.14 = bf16[1,32,8192]{2,1,0:T(8,128)(2,1)} copy(bf16[1,32,8192]{2,1,0:T(8,128)(2,1)} %bitcast.8) | data formatting | bytes 1048576
  97.5 1.3 %copy.15 = f32[512]{0:T(512)} copy(f32[512]{0:T(512)} %bitcast.12) | data formatting | bytes 4096

commit v5 on v4

--- a/solution.py
+++ b/solution.py
@@ -199,11 +199,11 @@
         kv_copies[i].wait()
 
         def part(j, sum_, i=i):
-            at = pl.ds(pl.multiple_of(i * step + j * 512, 512), 512)
+            at = pl.ds(pl.multiple_of(i * step + j * 1024, 1024), 1024)
             n = (hid[:, at].astype(F32) * inv * again[:, at]).astype(BF)
             return sum_ + dot(n, kvw[at, :])
 
-        fresh = lax.fori_loop(0, step // 512, part, fresh)
+        fresh = lax.fori_loop(0, step // 1024, part, fresh)
     fresh = fresh.astype(BF)
 
     for g in range(8):
@@ -570,7 +570,7 @@
                 acc[:, k * 256:(k + 1) * 256] += dot(gained, vv[k, at, :])
         return carry
 
-    lax.fori_loop(0, NZ, block, 0)
+    lax.fori_loop(0, NZ, block, 0, unroll=2)
     inv = lax.rsqrt(jnp.sum(ssq[...], axis=1, keepdims=True) / d_model + EPS)
     logits = acc[...] * inv
     top = jnp.max(logits, axis=1, keepdims=True)

time: 98.9 us -> 97.9 us (0.990)
  Pallas kernels: 95 us -> 94 us
    pallas_call x1, Pallas kernels: 95 us -> 94 us  [body(): pl.pallas_call(kernel, out_shape=(jax.ShapeDtypeStruct((TOK, d_model), BF...]
where the time goes in v5:
time: 97.9 us; the launch traced here: 97.7 us
  Pallas kernels  94 us (96%)
  local copies, waits for them, and re-layouts  3.12 us (3%)
    pallas_call x1, Pallas kernels, body(): pl.pallas_call(kernel, out_shape=(jax.ShapeDtypeStruct((TOK, d_model), BF...  94 us
    unnamed x2, local copies, waits for them, and re-layouts  3.12 us

profile of v5, /device:TPU:1, one launch (start us, length us, event | category | flops | bytes accessed | tf_op | source)
XLA Modules:
  0.0 97.7 jit_solution(13856300516589338253)
XLA Ops:
  0.6 94.0 %step.1 = (bf16[32,8192]{1,0:T(8,128)(2,1)}, f32[4,128]{1,0:T(4,128)}) custom-call(bf16[32,8192]{1,0:T(8,128)(2,1)} %bitcast.7, f32[1,8192]{1,0:T(1,128)} %bitcast.10, bf16[32,1024]{1,0:T(8,128)(2,1)} %bitcast.9, s32[32]{0:T(128)} %lens.1, s32[1,128]{1,0:T(1,128)} %bitcast.13, f32[1,8192]{1,0:T(1,128)} %bitcast.11, bf16[8192,256]{1,0:T(8,128)(2,1)} %kvw_h.1, ...), custom_call_target="tpu_custom_call" | custom-call | flops 4000000000 | bytes 24000000 | tf_op jit(solution)/shard_map/step/pallas_call | solution.py:737
  94.6 1.9 %copy.14 = bf16[1,32,8192]{2,1,0:T(8,128)(2,1)} copy(bf16[1,32,8192]{2,1,0:T(8,128)(2,1)} %bitcast.8) | data formatting | bytes 1048576
  96.5 1.3 %copy.15 = f32[512]{0:T(512)} copy(f32[512]{0:T(512)} %bitcast.12) | data formatting | bytes 4096
